TPU v7x, 512 devices: a whole 4x8x8 slice. The times are simulated.
512 devices in a mesh: dp: 8 (over z_lo, x), row: 8 (over z_hi, core), col: 8 (over y).
Axes of the slice: x: 4, y: 8, z: 8 (z_hi: 4, z_lo: 2; z = z_hi * 2 + z_lo), core: 2. Of those that a mesh axis runs over, the one named last changes fastest.
Arguments:
- inputs: bfloat16 [256, 16384], P(('dp', 'col'), 'row'), may hold values from -6 to 6
- cotangent: bfloat16 [256, 16384], P(('dp', 'col'), 'row'), may hold values from -3 to 3
- gate_weight: bfloat16 [16384, 8192], P('row', ('dp', 'col')), may hold values from -0.046875 to 0.046875
- up_weight: bfloat16 [16384, 8192], P('row', ('dp', 'col')), may hold values from -0.046875 to 0.046875
- down_weight: bfloat16 [8192, 16384], P(('dp', 'col'), 'row'), may hold values from -0.0625 to 0.0625
Outputs:
- grad_inputs: bfloat16 [256, 16384], P(('dp', 'col'), 'row')
- grad_gate_weight: bfloat16 [16384, 8192], P('row', ('dp', 'col'))
- grad_up_weight: bfloat16 [16384, 8192], P('row', ('dp', 'col'))
- grad_down_weight: bfloat16 [8192, 16384], P(('dp', 'col'), 'row')
All inputs are finite; a program needn't handle non-finite values.
Results may differ from a plain program's by a relative error of at most 0.0049.
Values may be sent and summed in bfloat16 or wider, within the bound.
No kernel may reach another device: no remote copies, remote signals or barrier semaphores. Data moves between devices by JAX's collectives and lax.ppermute only.
A program may use at most 64 MiB of HBM per device.

v0:
```python
import jax
import jax.numpy as jnp
from jax import lax
from jax.sharding import PartitionSpec as P


def swiglu_grads(summed, width):
    gate = summed[:, :width]
    up = summed[:, width : 2 * width]
    hidden_grad = summed[:, 2 * width :]
    sigma = jax.nn.sigmoid(gate)
    active = gate * sigma
    hidden = (active * up).astype(jnp.bfloat16)
    up_grad = (hidden_grad * active).astype(jnp.bfloat16)
    gate_grad = (hidden_grad * up * sigma * (1.0 + gate * (1.0 - sigma))).astype(jnp.bfloat16)
    return (hidden, gate_grad, up_grad)


def body(inputs, cotangent, gate_weight, up_weight, down_weight):
    gathered_in, gathered_cot = (
        lax.all_gather(inputs, ("dp", "col"), axis=0, tiled=True),
        lax.all_gather(cotangent, ("dp", "col"), axis=0, tiled=True),
    )
    width = gate_weight.shape[1]
    joined = jnp.concatenate([gate_weight, up_weight], axis=1)
    forward = jnp.dot(gathered_in, joined, preferred_element_type=jnp.float32)
    backward = lax.dot_general(
        gathered_cot, down_weight, (((1,), (1,)), ((), ())), preferred_element_type=jnp.float32
    )
    summed = lax.psum_scatter(
        jnp.concatenate([forward, backward], axis=1), "row", scatter_dimension=0, tiled=True
    )
    hidden, gate_grad, up_grad = swiglu_grads(summed, width)
    hidden, gate_grad, up_grad = (
        lax.all_gather(hidden, "row", axis=0, tiled=True),
        lax.all_gather(gate_grad, "row", axis=0, tiled=True),
        lax.all_gather(up_grad, "row", axis=0, tiled=True),
    )
    both_grads = jnp.concatenate([gate_grad, up_grad], axis=1)
    grad_inputs = lax.psum_scatter(
        lax.dot_general(
            both_grads, joined, (((1,), (1,)), ((), ())), preferred_element_type=jnp.float32
        ),
        ("dp", "col"),
        scatter_dimension=0,
        tiled=True,
    ).astype(jnp.bfloat16)
    contract_rows = (((0,), (0,)), ((), ()))
    grad_gate_weight = lax.dot_general(
        gathered_in, gate_grad, contract_rows, preferred_element_type=jnp.float32
    ).astype(jnp.bfloat16)
    grad_up_weight = lax.dot_general(
        gathered_in, up_grad, contract_rows, preferred_element_type=jnp.float32
    ).astype(jnp.bfloat16)
    grad_down_weight = lax.dot_general(
        hidden, gathered_cot, contract_rows, preferred_element_type=jnp.float32
    ).astype(jnp.bfloat16)
    return (grad_inputs, grad_gate_weight, grad_up_weight, grad_down_weight)


def solution(mesh):
    in_specs = (
        P(("dp", "col"), "row"),
        P(("dp", "col"), "row"),
        P("row", ("dp", "col")),
        P("row", ("dp", "col")),
        P(("dp", "col"), "row"),
    )
    out_specs = (
        P(("dp", "col"), "row"),
        P("row", ("dp", "col")),
        P("row", ("dp", "col")),
        P(("dp", "col"), "row"),
    )
    return jax.shard_map(body, mesh=mesh, in_specs=in_specs, out_specs=out_specs, check_vma=False)
```

profile of v0, /device:TPU:64, one launch (start us, length us, event | category | flops | bytes accessed | tf_op | source)
XLA Modules:
  0.0 1044.6 jit_solution(2122518229944774140)
XLA Ops:
  7.2 0.0 copy-start
  7.2 0.0 all-gather.7.cloned.1.call-start
  7.2 0.7 all-gather.7.cloned.1.call-update
  7.9 0.0 all-gather.5.cloned.1.call-start
  8.0 0.7 all-gather.5.cloned.1.call-update
  8.7 0.0 reduce-scatter.4.cloned.1.call-start
  8.7 1.9 constant_dynamic-update-slice_fusion.1
  10.6 1.9 constant_dynamic-update-slice_fusion
  12.5 300.1 %all-gather.7.cloned.1.call-done = bf16[64,4,2048]{2,1,0:T(4,128)(2,1)} async-done(((bf16[1,4,2048]{2,1,0:T(4,128)(2,1)}), bf16[64,4,2048]{2,1,0:T(4,128)(2,1)}) %all-gather.7.cloned.1.call-update) | async-done | bytes 1048592 | tf_op jit(solution)/shard_map/all_gather | solution.py:22
  312.6 1.3 reshape.11
  313.9 0.0 copy-done
  313.9 0.5 fusion.8
  314.4 297.2 %all-gather.5.cloned.1.call-done = bf16[64,4,2048]{2,1,0:T(4,128)(2,1)} async-done(((bf16[1,4,2048]{2,1,0:T(4,128)(2,1)}), bf16[64,4,2048]{2,1,0:T(4,128)(2,1)}) %all-gather.5.cloned.1.call-update) | async-done | bytes 1048592 | tf_op jit(solution)/shard_map/all_gather | solution.py:21
  611.7 1.3 reshape.9
  613.0 1.7 convolution_bitcast_fusion
  614.8 0.9 copy.21
  615.7 0.0 reduce-scatter.4.cloned.1.call-update
  615.7 1.3 dynamic-slice
  617.6 36.5 %reduce-scatter.4.cloned.1.call-done = f32[32,384]{1,0:T(8,128)} async-done(((f32[256,384]{1,0:T(8,128)}), f32[32,384]{1,0:T(8,128)}) %reduce-scatter.4.cloned.1.call-update) | async-done | bytes 49168 | tf_op jit(solution)/shard_map/reduce_scatter | solution.py:30
  654.1 0.8 multiply_convert_fusion
  654.9 14.5 %all_gather.18 = bf16[256,128]{1,0:T(8,128)(2,1)S(1)} all-gather(bf16[32,128]{1,0:T(8,128)(2,1)S(1)} %get-tuple-element.17), channel_id=1, replica_groups=mesh['dp'=8,'row'=8,'col'=8] {'row'}, dimensions={0}, use_global_device_ids=true | all-gather | bytes 73728 | tf_op jit(solution)/shard_map/all_gather | solution.py:37
  669.5 14.5 %all_gather.17 = bf16[256,128]{1,0:T(8,128)(2,1)S(1)} all-gather(bf16[32,128]{1,0:T(8,128)(2,1)S(1)} %get-tuple-element.18), channel_id=1, replica_groups=mesh['dp'=8,'row'=8,'col'=8] {'row'}, dimensions={0}, use_global_device_ids=true | all-gather | bytes 73728 | tf_op jit(solution)/shard_map/all_gather | solution.py:36
  684.0 0.3 fusion
  684.3 1.1 fusion.1
  685.5 0.0 copy-start.1
  685.5 3.1 fusion.2
  688.6 14.5 %all_gather.19 = bf16[256,128]{1,0:T(8,128)(2,1)S(1)} all-gather(bf16[32,128]{1,0:T(8,128)(2,1)S(1)} %get-tuple-element.16), channel_id=1, replica_groups=mesh['dp'=8,'row'=8,'col'=8] {'row'}, dimensions={0}, use_global_device_ids=true | all-gather | bytes 73728 | tf_op jit(solution)/shard_map/all_gather | solution.py:35
  703.1 1.1 convolution_convert_fusion
  704.2 0.0 copy-done.1
  704.2 1.0 copy.20
  705.2 1.0 copy.19
  706.2 331.2 %all-reduce.2 = bf16[256,2048]{1,0:T(8,128)(2,1)S(1)} all-reduce(f32[256,2048]{1,0:T(8,128)} %fusion.2), channel_id=3, replica_groups=mesh['dp'=8,'row'=8,'col'=8] {'dp','col'}, use_global_device_ids=true, to_apply=%region_1.0.clone | all-reduce | flops 524288 | bytes 3145728
  1037.5 0.6 dynamic-slice_convert_fusion
  (1 shorter events, 0.0 us)
Async XLA Ops:
  7.2 306.8 %copy-start = (bf16[128,2048]{1,0:T(8,128)(2,1)S(1)}, bf16[128,2048]{1,0:T(8,128)(2,1)}, u32[]{:S(2)}) copy-start(bf16[128,2048]{1,0:T(8,128)(2,1)} %param.9) | copy-start | bytes 1572868
  7.2 305.4 %all-gather.7.cloned.1.call-start = ((), (), s32[]{:S(2)}) async-start(), calls=%async_computation.2 | async-start | bytes 1064960 | tf_op jit(solution)/shard_map/all_gather | solution.py:22
  7.9 603.8 %all-gather.5.cloned.1.call-start = ((), (), s32[]{:S(2)}) async-start(), calls=%async_computation.1 | async-start | bytes 1064960 | tf_op jit(solution)/shard_map/all_gather | solution.py:21
  8.7 645.5 %reduce-scatter.4.cloned.1.call-start = ((), (), s32[]{:S(2)}) async-start(), calls=%async_computation.3 | async-start | bytes 442368 | tf_op jit(solution)/shard_map/reduce_scatter | solution.py:30
  685.5 18.8 %copy-start.1 = (bf16[2048,128]{0,1:T(8,128)(2,1)S(1)}, bf16[2048,128]{0,1:T(8,128)(2,1)}, u32[]{:S(2)}) copy-start(bf16[2048,128]{0,1:T(8,128)(2,1)} %fusion.1) | copy-start | bytes 1572868
Sparse Core Ops, SparseCore 0:
  10.1 302.4 all-gather.6
  314.7 296.9 all-gather.4
  615.8 38.2 reduce-scatter.3
where the time goes:
time: 1050 us; the launch traced here: 1040 us
  waiting for transfers between devices  635 us (60%)
  blocking collectives  375 us (36%)
  between operations  14.5 us (1%)
  local copies, waits for them, and re-layouts  11.3 us (1%)
    unnamed x1, blocking collectives  331 us
    all_gather x1, waiting for transfers between devices, body(): lax.all_gather(cotangent, ('dp', 'col'), axis=0, tiled=True)  300 us
    all_gather x1, waiting for transfers between devices, body(): lax.all_gather(inputs, ('dp', 'col'), axis=0, tiled=True)  297 us
    reduce_scatter x1, waiting for transfers between devices, body(): lax.psum_scatter(jnp.concatenate([forward, backward], axis=1), 'row', sca...  36.5 us
  transfers between devices with their start and end apart: 3, of which 3 were waited for; matrix products, arithmetic and copies ran while one was open for 1% of the time, Pallas kernels for 0%

commit v1 on v0

v1 whole, which is shorter than its diff:
```python
import jax
import jax.numpy as jnp
from jax import lax
from jax.sharding import PartitionSpec as P

GROUP = ("dp", "col")


def gather_rows(block, axes):
    n = lax.axis_size(axes)
    copies = jnp.broadcast_to(block[None], (n,) + block.shape)
    return lax.all_to_all(copies, axes, split_axis=0, concat_axis=0, tiled=True)


def swiglu_grads(summed, width):
    gate = summed[:, :width]
    up = summed[:, width : 2 * width]
    hidden_grad = summed[:, 2 * width :]
    sigma = jax.nn.sigmoid(gate)
    active = gate * sigma
    hidden = (active * up).astype(jnp.bfloat16)
    up_grad = (hidden_grad * active).astype(jnp.bfloat16)
    gate_grad = (hidden_grad * up * sigma * (1.0 + gate * (1.0 - sigma))).astype(jnp.bfloat16)
    return (hidden, gate_grad, up_grad)


def body(inputs, cotangent, gate_weight, up_weight, down_weight):
    depth, width = gate_weight.shape
    groups = lax.axis_size(GROUP)
    rows = lax.axis_size("row")
    tokens = inputs.shape[0] * groups
    gathered_in = gather_rows(inputs, GROUP).reshape(tokens, depth)
    gathered_cot = gather_rows(cotangent, GROUP).reshape(tokens, depth)
    joined = jnp.concatenate([gate_weight, up_weight], axis=1)
    forward = jnp.dot(gathered_in, joined, preferred_element_type=jnp.float32)
    backward = lax.dot_general(
        gathered_cot, down_weight, (((1,), (1,)), ((), ())), preferred_element_type=jnp.float32
    )
    partial = jnp.concatenate([forward, backward], axis=1).reshape(rows, tokens // rows, 3 * width)
    summed = jnp.sum(lax.all_to_all(partial, "row", split_axis=0, concat_axis=0, tiled=True), axis=0)
    triple = jnp.concatenate(swiglu_grads(summed, width), axis=1)
    triple = lax.all_gather(triple, "row", axis=0, tiled=True)
    hidden = triple[:, :width]
    both_grads = triple[:, width:]
    partial_in = lax.dot_general(
        both_grads, joined, (((1,), (1,)), ((), ())), preferred_element_type=jnp.float32
    ).astype(jnp.bfloat16)
    pieces = lax.all_to_all(
        partial_in.reshape(groups, tokens // groups, depth), GROUP, split_axis=0, concat_axis=0, tiled=True
    )
    grad_inputs = jnp.sum(pieces.astype(jnp.float32), axis=0).astype(jnp.bfloat16)
    contract_rows = (((0,), (0,)), ((), ()))
    grad_gate_weight = lax.dot_general(
        gathered_in, both_grads[:, :width], contract_rows, preferred_element_type=jnp.float32
    ).astype(jnp.bfloat16)
    grad_up_weight = lax.dot_general(
        gathered_in, both_grads[:, width:], contract_rows, preferred_element_type=jnp.float32
    ).astype(jnp.bfloat16)
    grad_down_weight = lax.dot_general(
        hidden, gathered_cot, contract_rows, preferred_element_type=jnp.float32
    ).astype(jnp.bfloat16)
    return (grad_inputs, grad_gate_weight, grad_up_weight, grad_down_weight)


def solution(mesh):
    in_specs = (
        P(("dp", "col"), "row"),
        P(("dp", "col"), "row"),
        P("row", ("dp", "col")),
        P("row", ("dp", "col")),
        P(("dp", "col"), "row"),
    )
    out_specs = (
        P(("dp", "col"), "row"),
        P("row", ("dp", "col")),
        P("row", ("dp", "col")),
        P(("dp", "col"), "row"),
    )
    return jax.shard_map(body, mesh=mesh, in_specs=in_specs, out_specs=out_specs, check_vma=False)
```

time: 1050 us -> 166 us (0.16)
  the two profiles are of different devices: /device:TPU:64 before, /device:TPU:8 now
where the time goes in v1:
time: 166 us; the launch traced here: 165 us
  blocking collectives  81 us (49%)
  waiting for transfers between devices  51.9 us (31%)
  starting transfers between devices  11.4 us (7%)
  local copies, waits for them, and re-layouts  10.9 us (7%)
  matrix products  6.64 us (4%)
  other arithmetic  2.36 us (1%)
    all_to_all x1, blocking collectives, gather_rows(): return lax.all_to_all(copies, axes, split_axis=0, concat_axis=0, tiled=True)  41.6 us
    all_to_all x1, waiting for transfers between devices, body(): lax.all_to_all(partial_in.reshape(groups, tokens // groups, depth), GROUP...  26.3 us
    all_to_all x1, waiting for transfers between devices, gather_rows(): return lax.all_to_all(copies, axes, split_axis=0, concat_axis=0, tiled=True)  25.6 us
    all_to_all x1, blocking collectives, body(): lax.all_to_all(partial, 'row', split_axis=0, concat_axis=0, tiled=True)  24.8 us
    all_gather x1, blocking collectives, body(): triple = lax.all_gather(triple, 'row', axis=0, tiled=True)  14.7 us
    all_to_all x1, starting transfers between devices, gather_rows(): return lax.all_to_all(copies, axes, split_axis=0, concat_axis=0, tiled=True)  5.91 us
    all_to_all x1, starting transfers between devices, body(): lax.all_to_all(partial_in.reshape(groups, tokens // groups, depth), GROUP...  5.47 us
  transfers between devices with their start and end apart: 2, of which 2 were waited for; matrix products, arithmetic and copies ran while one was open for 4% of the time, Pallas kernels for 0%

profile of v1, /device:TPU:8, one launch (start us, length us, event | category | flops | bytes accessed | tf_op | source)
XLA Modules:
  0.0 165.0 jit_solution(4662748611106344497)
XLA Ops:
  0.6 0.0 copy-start
  0.6 1.3 broadcast_in_dim.5
  1.9 0.0 copy-start.3
  1.9 41.6 %all_to_all.20 = bf16[64,4,2048]{2,1,0:T(4,128)(2,1)S(1)} all-to-all(bf16[64,4,2048]{2,1,0:T(4,128)(2,1)S(1)} %broadcast_in_dim.5), channel_id=1, replica_groups=mesh['dp'=8,'row'=8,'col'=8] {'dp','col'}, dimensions={0} | all-to-all | bytes 2097152 | tf_op jit(solution)/shard_map/all_to_all | solution.py:12
  43.5 0.0 copy-done.3
  43.5 1.5 broadcast_in_dim.4
  45.0 0.0 copy-start.1
  45.0 5.9 %all-to-all-start = ((bf16[64,4,2048]{2,1,0:T(4,128)(2,1)}), bf16[64,4,2048]{2,1,0:T(4,128)(2,1)}, u32[]{:S(2)}, u32[]{:S(2)}) async-start(bf16[64,4,2048]{2,1,0:T(4,128)(2,1)} %broadcast_in_dim.4), calls=%async_computation | async-start | bytes 2097152 | tf_op jit(solution)/shard_map/all_to_all | solution.py:12
  50.9 0.0 copy-done.1
  50.9 0.0 copy-start.2
  51.0 0.8 constant_dynamic-update-slice_fusion.1
  51.8 0.4 copy-done.2
  52.2 0.9 constant_dynamic-update-slice_fusion
  53.0 0.3 reshape.23
  53.3 0.0 copy-done
  53.3 0.5 fusion.7
  53.8 25.6 %all-to-all-done = bf16[64,4,2048]{2,1,0:T(4,128)(2,1)} async-done(((bf16[64,4,2048]{2,1,0:T(4,128)(2,1)}), bf16[64,4,2048]{2,1,0:T(4,128)(2,1)}, u32[]{:S(2)}, u32[]{:S(2)}) %all-to-all-start) | async-done | bytes 1048608 | tf_op jit(solution)/shard_map/all_to_all | solution.py:12
  79.4 1.3 reshape.22
  80.7 1.7 %convolution_bitcast_fusion = f32[256,256]{0,1:T(8,128)S(1)} fusion(bf16[2048,256]{1,0:T(8,128)(2,1)} %constant_dynamic-update-slice_fusion, bf16[256,2048]{1,0:T(8,128)(2,1)S(1)} %reshape.22), kind=kOutput, calls=%fused_computation.6 | convolution fusion | flops 268435456 | bytes 2359296 | tf_op jit(solution)/shard_map/dot_general | solution.py:35
  82.5 0.2 copy.11
  82.7 24.8 %all_to_all.21 = f32[8,32,384]{2,1,0:T(8,128)S(1)} all-to-all(f32[8,32,384]{2,1,0:T(8,128)S(1)} %bitcast.15), channel_id=1, replica_groups=mesh['dp'=8,'row'=8,'col'=8] {'row'}, dimensions={0} | all-to-all | bytes 786432 | tf_op jit(solution)/shard_map/all_to_all | solution.py:40
  107.5 14.7 %all_gather.3 = bf16[256,384]{1,0:T(8,128)(2,1)S(1)} all-gather(bf16[32,384]{1,0:T(8,128)(2,1)S(1)} %pad_maximum_fusion.1), channel_id=1, replica_groups=mesh['dp'=8,'row'=8,'col'=8] {'row'}, dimensions={0}, use_global_device_ids=true | all-gather | bytes 221184 | tf_op jit(solution)/shard_map/all_gather | solution.py:42
  122.2 2.7 %convolution_convert_fusion = bf16[256,2048]{1,0:T(8,128)(2,1)} fusion(bf16[2048,256]{1,0:T(8,128)(2,1)} %constant_dynamic-update-slice_fusion, bf16[256,384]{1,0:T(8,128)(2,1)S(1)} %all_gather.3), kind=kOutput, calls=%fused_computation | convolution fusion | flops 268959744 | bytes 2228224 | tf_op jit(solution)/shard_map/dot_general | solution.py:45
  124.9 2.3 %reshape.25 = bf16[64,4,2048]{2,1,0:T(4,128)(2,1)} reshape(bf16[256,2048]{1,0:T(8,128)(2,1)} %convolution_convert_fusion) | data formatting | bytes 2097152 | tf_op jit(solution)/shard_map/reshape | solution.py:49
  127.1 5.5 %all-to-all-start.3 = ((bf16[64,4,2048]{2,1,0:T(4,128)(2,1)}), bf16[64,4,2048]{2,1,0:T(4,128)(2,1)}, u32[]{:S(2)}, u32[]{:S(2)}) async-start(bf16[64,4,2048]{2,1,0:T(4,128)(2,1)} %reshape.25), calls=%async_computation.3 | async-start | bytes 2097152 | tf_op jit(solution)/shard_map/all_to_all | solution.py:48
  132.6 0.3 fusion
  132.9 1.0 copy.12
  133.9 0.3 fusion.1
  134.3 1.0 copy.13
  135.3 1.1 convolution_convert_fusion.1
  136.4 26.3 %all-to-all-done.3 = bf16[64,4,2048]{2,1,0:T(4,128)(2,1)} async-done(((bf16[64,4,2048]{2,1,0:T(4,128)(2,1)}), bf16[64,4,2048]{2,1,0:T(4,128)(2,1)}, u32[]{:S(2)}, u32[]{:S(2)}) %all-to-all-start.3) | async-done | bytes 1048608 | tf_op jit(solution)/shard_map/all_to_all | solution.py:48
  162.7 2.3 %reduce_sum.22 = bf16[4,2048]{1,0:T(4,128)(2,1)} reduce(bf16[64,4,2048]{2,1,0:T(4,128)(2,1)} %all-to-all-done.3, bf16[]{:T(256)} %constant.5.clone.1), dimensions={0}, to_apply=%region_1.0 | reduce | flops 516096 | bytes 1064962 | tf_op jit(solution)/shard_map/reduce_sum | solution.py:51
  (4 shorter events, 0.1 us)
Async XLA Ops:
  0.6 52.7 %copy-start = (bf16[128,2048]{1,0:T(8,128)(2,1)S(1)}, bf16[128,2048]{1,0:T(8,128)(2,1)}, u32[]{:S(2)}) copy-start(bf16[128,2048]{1,0:T(8,128)(2,1)} %param.9) | copy-start | bytes 1572868
  1.9 41.6 %copy-start.3 = (bf16[4,2048]{1,0:T(4,128)(2,1)S(1)}, bf16[4,2048]{1,0:T(4,128)(2,1)}, u32[]{:S(2)}) copy-start(bf16[4,2048]{1,0:T(4,128)(2,1)} %param.5) | copy-start | bytes 49156
  45.0 5.9 %copy-start.1 = (bf16[2048,128]{1,0:T(8,128)(2,1)S(1)}, bf16[2048,128]{1,0:T(8,128)(2,1)}, u32[]{:S(2)}) copy-start(bf16[2048,128]{1,0:T(8,128)(2,1)} %param.7) | copy-start | bytes 1572868
  45.0 34.4 %all-to-all-start = ((bf16[64,4,2048]{2,1,0:T(4,128)(2,1)}), bf16[64,4,2048]{2,1,0:T(4,128)(2,1)}, u32[]{:S(2)}, u32[]{:S(2)}) async-start(bf16[64,4,2048]{2,1,0:T(4,128)(2,1)} %broadcast_in_dim.4), calls=%async_computation | async-start | bytes 2097152 | tf_op jit(solution)/shard_map/all_to_all | solution.py:12
  50.9 1.2 copy-start.2
  127.1 35.6 %all-to-all-start.3 = ((bf16[64,4,2048]{2,1,0:T(4,128)(2,1)}), bf16[64,4,2048]{2,1,0:T(4,128)(2,1)}, u32[]{:S(2)}, u32[]{:S(2)}) async-start(bf16[64,4,2048]{2,1,0:T(4,128)(2,1)} %reshape.25), calls=%async_computation.3 | async-start | bytes 2097152 | tf_op jit(solution)/shard_map/all_to_all | solution.py:48

commit v2 on v1

v2 whole, which is shorter than its diff:
```python
import jax
import jax.numpy as jnp
from jax import lax
from jax.sharding import Mesh
from jax.sharding import PartitionSpec as P

DP = ("z_lo", "x")
GROUP = ("z_lo", "x", "col")
ROW = ("z_hi", "core")


def exchange(pieces, axes):
    return lax.all_to_all(pieces, axes, split_axis=0, concat_axis=0, tiled=True)


def spread(block, axes):
    n = lax.axis_size(axes)
    return exchange(jnp.broadcast_to(block[None], (n,) + block.shape), axes)


def swiglu_grads(summed, width):
    gate = summed[:, :width]
    up = summed[:, width : 2 * width]
    hidden_grad = summed[:, 2 * width :]
    sigma = jax.nn.sigmoid(gate)
    active = gate * sigma
    hidden = (active * up).astype(jnp.bfloat16)
    up_grad = (hidden_grad * active).astype(jnp.bfloat16)
    gate_grad = (hidden_grad * up * sigma * (1.0 + gate * (1.0 - sigma))).astype(jnp.bfloat16)
    return (hidden, gate_grad, up_grad)


def body(inputs, cotangent, gate_weight, up_weight, down_weight):
    own, depth = inputs.shape
    width = gate_weight.shape[1]
    columns = lax.axis_size("col")
    planes = lax.axis_size(DP)
    groups = columns * planes
    tokens = own * groups

    line = spread(jnp.concatenate([inputs, cotangent], axis=0), "col")
    line = line.reshape(columns, 2, own, depth).transpose(1, 0, 2, 3).reshape(2 * columns * own, depth)
    plane = spread(line, DP).reshape(planes, 2, columns * own, depth)
    gathered_in = plane[:, 0].reshape(tokens, depth)
    gathered_cot = plane[:, 1].reshape(tokens, depth)

    joined = jnp.concatenate([gate_weight, up_weight], axis=1)
    forward = jnp.dot(gathered_in, joined, preferred_element_type=jnp.float32)
    backward = lax.dot_general(
        gathered_cot, down_weight, (((1,), (1,)), ((), ())), preferred_element_type=jnp.float32
    )
    halves = jnp.concatenate([forward, backward], axis=1).reshape(2, tokens // 2, 3 * width)
    core = lax.axis_index("core")
    mine = lax.dynamic_index_in_dim(halves, core, 0, keepdims=False)
    other = lax.dynamic_index_in_dim(halves, 1 - core, 0, keepdims=False)
    pair = mine + lax.ppermute(other, "core", [(0, 1), (1, 0)])
    summed = jnp.sum(spread(pair, "z_hi"), axis=0)
    triple = jnp.concatenate(swiglu_grads(summed, width), axis=1)
    triple = lax.all_gather(triple, "core", axis=0, tiled=True)
    hidden = triple[:, :width]
    both_grads = triple[:, width:]

    partial_in = lax.dot_general(
        both_grads, joined, (((1,), (1,)), ((), ())), preferred_element_type=jnp.float32
    ).astype(jnp.bfloat16)
    pieces = exchange(partial_in.reshape(groups, own, depth), GROUP)
    grad_inputs = jnp.sum(pieces.astype(jnp.float32), axis=0).astype(jnp.bfloat16)
    contract_rows = (((0,), (0,)), ((), ()))
    grad_gate_weight = lax.dot_general(
        gathered_in, both_grads[:, :width], contract_rows, preferred_element_type=jnp.float32
    ).astype(jnp.bfloat16)
    grad_up_weight = lax.dot_general(
        gathered_in, both_grads[:, width:], contract_rows, preferred_element_type=jnp.float32
    ).astype(jnp.bfloat16)
    grad_down_weight = lax.dot_general(
        hidden, gathered_cot, contract_rows, preferred_element_type=jnp.float32
    ).astype(jnp.bfloat16)
    return (grad_inputs, grad_gate_weight, grad_up_weight, grad_down_weight)


def solution(mesh):
    fine = Mesh(mesh.devices.reshape(2, 4, 4, 2, 8), ("z_lo", "x", "z_hi", "core", "col"))
    in_specs = (P(GROUP, ROW), P(GROUP, ROW), P(ROW, GROUP), P(ROW, GROUP), P(GROUP, ROW))
    out_specs = (P(GROUP, ROW), P(ROW, GROUP), P(ROW, GROUP), P(GROUP, ROW))
    return jax.shard_map(body, mesh=fine, in_specs=in_specs, out_specs=out_specs, check_vma=False)
```

time: 166 us -> 141 us (0.85)
  blocking collectives: 81 us -> 50.3 us
  starting transfers between devices: 11.4 us -> 17.2 us
  waiting for transfers between devices: 51.9 us -> 48 us
  other arithmetic: 2.36 us -> 4.83 us
  matrix products: 6.64 us -> 8.58 us
    all_to_all x2, blocking collectives: 66.3 us -> 48.3 us  [exchange(): return lax.all_to_all(pieces, axes, split_axis=0, concat_axis=0, tiled=True)]
    all_gather x1, blocking collectives: 14.7 us -> 1.95 us  [body(): triple = lax.all_gather(triple, 'core', axis=0, tiled=True)]
    all_to_all x2, waiting for transfers between devices: 51.9 us -> 46.6 us  [exchange(): return lax.all_to_all(pieces, axes, split_axis=0, concat_axis=0, tiled=True)]
    all_to_all x2, starting transfers between devices: 11.4 us -> 15.3 us  [exchange(): return lax.all_to_all(pieces, axes, split_axis=0, concat_axis=0, tiled=True)]
    ppermute x0 -> x1, starting transfers between devices: none -> 1.92 us  [body(): pair = mine + lax.ppermute(other, 'core', [(0, 1), (1, 0)])]
    slice x0 -> x1, local copies, waits for them, and re-layouts: none -> 1.68 us  [body(): gathered_in = plane[:, 0].reshape(tokens, depth)]
    reshape x3 -> x2, local copies, waits for them, and re-layouts: 3.85 us -> 2.41 us  [the longest x1 2.25 us: body(): pieces = exchange(partial_in.reshape(groups, own, depth), GROUP)]
  transfers between devices with their start and end apart: 2 -> 3, of which waited for: 2 -> 3; matrix products, arithmetic and copies ran while one was open for 4% -> 5% of each run, Pallas kernels for 0% -> 0%
where the time goes in v2:
time: 141 us; the launch traced here: 140 us
  blocking collectives  50.3 us (36%)
  waiting for transfers between devices  48 us (34%)
  starting transfers between devices  17.2 us (12%)
  local copies, waits for them, and re-layouts  10.3 us (7%)
  matrix products  8.58 us (6%)
  other arithmetic  4.83 us (3%)
    all_to_all x2, blocking collectives, exchange(): return lax.all_to_all(pieces, axes, split_axis=0, concat_axis=0, tiled=True)  48.3 us
    all_to_all x2, waiting for transfers between devices, exchange(): return lax.all_to_all(pieces, axes, split_axis=0, concat_axis=0, tiled=True)  46.6 us
    all_to_all x2, starting transfers between devices, exchange(): return lax.all_to_all(pieces, axes, split_axis=0, concat_axis=0, tiled=True)  15.3 us
  transfers between devices with their start and end apart: 3, of which 3 were waited for; matrix products, arithmetic and copies ran while one was open for 5% of the time, Pallas kernels for 0%

profile of v2, /device:TPU:8, one launch (start us, length us, event | category | flops | bytes accessed | tf_op | source)
XLA Modules:
  0.0 140.0 jit_solution(8688353329030488741)
XLA Ops:
  0.6 0.0 copy-start
  0.6 0.8 pad_maximum_fusion.2
  1.5 17.8 %all_to_all.20 = bf16[8,8,2048]{2,1,0:T(8,128)(2,1)S(1)} all-to-all(bf16[8,8,2048]{2,1,0:T(8,128)(2,1)S(1)} %broadcast_in_dim.8), channel_id=1, replica_groups=mesh['z_lo'=2,'x'=4,'z_hi'=4,'core'=2,'col'=8] {'col'}, dimensions={0} | all-to-all | bytes 524288 | tf_op jit(solution)/shard_map/all_to_all | solution.py:13
  19.3 0.1 copy.18
  19.4 0.2 copy.19
  19.6 0.1 broadcast_in_dim.9
  19.7 1.6 %broadcast_in_dim.10 = bf16[8,64,2048]{2,1,0:T(8,128)(2,1)} broadcast(bf16[64,2048]{1,0:T(8,128)(2,1)S(1)} %broadcast_in_dim.9), dimensions={1,2} | broadcast | bytes 2359296 | tf_op jit(solution)/shard_map/broadcast_in_dim | solution.py:18
  21.3 0.0 copy-start.2
  21.3 6.2 %all-to-all-start.1 = ((bf16[8,64,2048]{2,1,0:T(8,128)(2,1)}), bf16[8,64,2048]{2,1,0:T(8,128)(2,1)S(1)}, u32[]{:S(2)}, u32[]{:S(2)}) async-start(bf16[8,64,2048]{2,1,0:T(8,128)(2,1)} %broadcast_in_dim.10), calls=%async_computation.1 | async-start | bytes 4194304 | tf_op jit(solution)/shard_map/all_to_all | solution.py:13
  27.5 0.0 copy-done.2
  27.5 0.9 constant_dynamic-update-slice_fusion.1
  28.4 1.9 %constant_dynamic-update-slice_fusion = bf16[2048,256]{1,0:T(8,128)(2,1)} fusion(bf16[2048,256]{1,0:T(8,128)(2,1)} %constant_dynamic-update-slice_fusion.1, bf16[2048,128]{1,0:T(8,128)(2,1)} %param.8), kind=kLoop, calls=%fused_computation.18 | loop fusion | bytes 1048576 | tf_op jit(solution)/shard_map/concatenate | solution.py:47
  30.3 20.7 %all-to-all-done.1 = bf16[8,64,2048]{2,1,0:T(8,128)(2,1)S(1)} async-done(((bf16[8,64,2048]{2,1,0:T(8,128)(2,1)}), bf16[8,64,2048]{2,1,0:T(8,128)(2,1)S(1)}, u32[]{:S(2)}, u32[]{:S(2)}) %all-to-all-start.1) | async-done | bytes 2097184 | tf_op jit(solution)/shard_map/all_to_all | solution.py:13
  51.0 0.0 copy-start.1
  51.0 1.3 copy-done.1
  52.3 1.7 %fusion.5 = (bf16[8,1,32,2048]{3,2,1,0:T(8,128)(2,1)S(1)}, bf16[8,1,32,2048]{3,2,1,0:T(8,128)(2,1)S(1)}) fusion(bf16[8,2,32,2048]{3,2,1,0:T(8,128)(2,1)} %bitcast.24), kind=kLoop, calls=%fused_computation.20 | loop fusion | bytes 4194304 | tf_op jit(solution)/shard_map/slice | solution.py:44
  54.0 1.7 %fusion.6 = f32[256,256]{0,1:T(8,128)S(1)} fusion(bf16[256,2048]{1,0:T(8,128)(2,1)S(1)} %bitcast.19, bf16[2048,256]{1,0:T(8,128)(2,1)} %constant_dynamic-update-slice_fusion), kind=kOutput, calls=%fused_computation.21 | convolution fusion | flops 268435456 | bytes 2359296 | tf_op jit(solution)/shard_map/dot_general | solution.py:48
  55.7 0.0 copy-done
  55.7 0.5 fusion.7
  56.3 0.2 copy.22
  56.5 1.9 %collective-permute-start = (f32[128,384]{1,0:T(8,128)S(1)}, f32[128,384]{1,0:T(8,128)S(1)}, u32[]{:S(2)}, u32[]{:S(2)}) collective-permute-start(f32[128,384]{1,0:T(8,128)S(1)} %dynamic-slice_bitcast_fusion), channel_id=1, source_target_pairs={{0,8},{8,0},{1,9},{9,1},{2,10},{10,2},{3,11},{11,3},{4,12},{12,4},... | collective-permute-start | bytes 589832 | tf_op jit(solution)/shard_map/ppermute | solution.py:56
  58.4 1.4 %collective-permute-done = f32[128,384]{1,0:T(8,128)S(1)} collective-permute-done((f32[128,384]{1,0:T(8,128)S(1)}, f32[128,384]{1,0:T(8,128)S(1)}, u32[]{:S(2)}, u32[]{:S(2)}) %collective-permute-start) | collective-permute-done | bytes 196640 | tf_op jit(solution)/shard_map/ppermute | solution.py:56
  59.8 0.1 broadcast_in_dim.22
  59.9 30.6 %all_to_all.21 = f32[4,128,384]{2,1,0:T(8,128)S(1)} all-to-all(f32[4,128,384]{2,1,0:T(8,128)S(1)} %broadcast_in_dim.22), channel_id=1, replica_groups=mesh['z_lo'=2,'x'=4,'z_hi'=4,'core'=2,'col'=8] {'z_hi'}, dimensions={0} | all-to-all | bytes 1572864 | tf_op jit(solution)/shard_map/all_to_all | solution.py:13
  90.5 0.7 reduce_sum.21
  91.2 1.0 multiply_convert_fusion.2
  92.2 1.9 %all_gather.3 = bf16[256,384]{1,0:T(8,128)(2,1)S(1)} all-gather(bf16[128,384]{1,0:T(8,128)(2,1)S(1)} %pad_maximum_fusion.1), channel_id=1, replica_groups=mesh['z_lo'=2,'x'=4,'z_hi'=4,'core'=2,'col'=8] {'core'}, dimensions={0}, use_global_device_ids=true | all-gather | bytes 294912 | tf_op jit(solution)/shard_map/all_gather | solution.py:59
  94.1 2.7 %convolution_convert_fusion = bf16[256,2048]{1,0:T(8,128)(2,1)} fusion(bf16[2048,256]{1,0:T(8,128)(2,1)} %constant_dynamic-update-slice_fusion, bf16[256,384]{1,0:T(8,128)(2,1)S(1)} %all_gather.3), kind=kOutput, calls=%fused_computation | convolution fusion | flops 268959744 | bytes 2228224 | tf_op jit(solution)/shard_map/dot_general | solution.py:63
  96.8 2.2 %reshape.26 = bf16[64,4,2048]{2,1,0:T(4,128)(2,1)} reshape(bf16[256,2048]{1,0:T(8,128)(2,1)} %convolution_convert_fusion) | data formatting | bytes 2097152 | tf_op jit(solution)/shard_map/reshape | solution.py:66
  99.0 9.1 %all-to-all-start.3 = ((bf16[64,4,2048]{2,1,0:T(4,128)(2,1)}), bf16[64,4,2048]{2,1,0:T(4,128)(2,1)}, u32[]{:S(2)}, u32[]{:S(2)}) async-start(bf16[64,4,2048]{2,1,0:T(4,128)(2,1)} %reshape.26), calls=%async_computation.3 | async-start | bytes 2097152 | tf_op jit(solution)/shard_map/all_to_all | solution.py:13
  108.1 1.1 convolution_convert_fusion.1
  109.2 1.3 convolution_convert_fusion.2
  110.5 1.3 convolution_convert_fusion.3
  111.8 25.9 %all-to-all-done.3 = bf16[64,4,2048]{2,1,0:T(4,128)(2,1)} async-done(((bf16[64,4,2048]{2,1,0:T(4,128)(2,1)}), bf16[64,4,2048]{2,1,0:T(4,128)(2,1)}, u32[]{:S(2)}, u32[]{:S(2)}) %all-to-all-start.3) | async-done | bytes 1048608 | tf_op jit(solution)/shard_map/all_to_all | solution.py:13
  137.7 2.3 %reduce_sum.22 = bf16[4,2048]{1,0:T(4,128)(2,1)} reduce(bf16[64,4,2048]{2,1,0:T(4,128)(2,1)} %all-to-all-done.3, bf16[]{:T(256)} %constant.23.clone.1), dimensions={0}, to_apply=%region_1.2 | reduce | flops 516096 | bytes 1064962 | tf_op jit(solution)/shard_map/reduce_sum | solution.py:67
  (5 shorter events, 0.1 us)
Async XLA Ops:
  0.6 55.1 %copy-start = (bf16[128,2048]{1,0:T(8,128)(2,1)S(1)}, bf16[128,2048]{1,0:T(8,128)(2,1)}, u32[]{:S(2)}) copy-start(bf16[128,2048]{1,0:T(8,128)(2,1)} %param.9) | copy-start | bytes 1572868
  21.3 6.2 %copy-start.2 = (bf16[2048,128]{1,0:T(8,128)(2,1)S(1)}, bf16[2048,128]{1,0:T(8,128)(2,1)}, u32[]{:S(2)}) copy-start(bf16[2048,128]{1,0:T(8,128)(2,1)} %param.7) | copy-start | bytes 1572868
  21.3 29.7 %all-to-all-start.1 = ((bf16[8,64,2048]{2,1,0:T(8,128)(2,1)}), bf16[8,64,2048]{2,1,0:T(8,128)(2,1)S(1)}, u32[]{:S(2)}, u32[]{:S(2)}) async-start(bf16[8,64,2048]{2,1,0:T(8,128)(2,1)} %broadcast_in_dim.10), calls=%async_computation.1 | async-start | bytes 4194304 | tf_op jit(solution)/shard_map/all_to_all | solution.py:13
  51.0 1.3 copy-start.1
  56.5 3.3 %collective-permute-start = (f32[128,384]{1,0:T(8,128)S(1)}, f32[128,384]{1,0:T(8,128)S(1)}, u32[]{:S(2)}, u32[]{:S(2)}) collective-permute-start(f32[128,384]{1,0:T(8,128)S(1)} %dynamic-slice_bitcast_fusion), channel_id=1, source_target_pairs={{0,8},{8,0},{1,9},{9,1},{2,10},{10,2},{3,11},{11,3},{4,12},{12,4},... | collective-permute-start | bytes 589832 | tf_op jit(solution)/shard_map/ppermute | solution.py:56
  99.0 38.6 %all-to-all-start.3 = ((bf16[64,4,2048]{2,1,0:T(4,128)(2,1)}), bf16[64,4,2048]{2,1,0:T(4,128)(2,1)}, u32[]{:S(2)}, u32[]{:S(2)}) async-start(bf16[64,4,2048]{2,1,0:T(4,128)(2,1)} %reshape.26), calls=%async_computation.3 | async-start | bytes 2097152 | tf_op jit(solution)/shard_map/all_to_all | solution.py:13

commit v3 on v2

v3 whole, which is shorter than its diff:
```python
import functools

import jax
import jax.numpy as jnp
from jax import lax
from jax.experimental import pallas as pl
from jax.experimental.pallas import tpu as pltpu
from jax.sharding import Mesh
from jax.sharding import PartitionSpec as P

DP = ("z_lo", "x")
GROUP = ("z_lo", "x", "col")
ROW = ("z_hi", "core")
LIMIT = 40 * 1024 * 1024
F32 = jnp.float32
BF16 = jnp.bfloat16
LAST = (((1,), (1,)), ((), ()))
FIRST = (((0,), (0,)), ((), ()))


def exchange(pieces, axes):
    return lax.all_to_all(pieces, axes, split_axis=0, concat_axis=0, tiled=True)


def spread(block, axes):
    n = lax.axis_size(axes)
    return exchange(jnp.broadcast_to(block[None], (n,) + block.shape), axes)


def call(kernel, out_shape, cost, **rest):
    flops, size = cost
    return pl.pallas_call(
        kernel,
        out_shape=out_shape,
        cost_estimate=pl.CostEstimate(flops=flops, bytes_accessed=size, transcendentals=0),
        compiler_params=pltpu.CompilerParams(vmem_limit_bytes=LIMIT),
        **rest,
    )


def upper(shape):
    return lax.broadcasted_iota(jnp.int32, shape, len(shape) - 2) < 4


def split_line(line_ref, out_ref, kept, sems):
    columns, _, depth = line_ref.shape
    blocks = line_ref[...].astype(F32)
    top = upper((8, depth))
    inputs, cotangents = [], []
    for j in range(columns // 2):
        a, b = blocks[2 * j], blocks[2 * j + 1]
        inputs.append(jnp.where(top, a, pltpu.roll(b, 4, 0)))
        cotangents.append(jnp.where(top, pltpu.roll(a, 4, 0), b))
    kept[...] = jnp.concatenate(inputs + cotangents, axis=0).astype(BF16)
    copies = [pltpu.make_async_copy(kept, out_ref.at[p], sems.at[p]) for p in range(out_ref.shape[0])]
    for copy in copies:
        copy.start()
    for copy in copies:
        copy.wait()


def forward(which_ref, plane_ref, gate_ref, up_ref, down_ref, out_ref):
    planes, rows, depth = plane_ref.shape
    half = rows // 2
    width = gate_ref.shape[1]
    inputs = plane_ref[:, :half, :].reshape(planes * half, depth)
    cotangents = plane_ref[:, half:, :].reshape(planes * half, depth)
    joined = jnp.concatenate([gate_ref[...], up_ref[...]], axis=1)
    out_ref[:, : 2 * width] = jnp.dot(inputs, joined, preferred_element_type=F32)
    out_ref[:, 2 * width :] = lax.dot_general(cotangents, down_ref[...], LAST, preferred_element_type=F32)


def run_forward(which, plane, gate_weight, up_weight, down_weight):
    planes, rows, depth = plane.shape
    width = gate_weight.shape[1]
    tokens = planes * rows // 4
    whole = lambda i, c: (0, 0)
    return call(
        forward,
        jax.ShapeDtypeStruct((tokens, 3 * width), F32),
        (6 * tokens * depth * width, plane.size + 6 * depth * width),
        grid_spec=pltpu.PrefetchScalarGridSpec(
            num_scalar_prefetch=1,
            grid=(1,),
            in_specs=[
                pl.BlockSpec((planes // 2, rows, depth), lambda i, c: (c[0], 0, 0)),
                pl.BlockSpec(gate_weight.shape, whole),
                pl.BlockSpec(up_weight.shape, whole),
                pl.BlockSpec(down_weight.shape, whole),
            ],
            out_specs=pl.BlockSpec((tokens, 3 * width), whole),
        ),
    )(which, plane, gate_weight, up_weight, down_weight)


def activate(parts_ref, out_ref):
    width = out_ref.shape[1] // 3
    summed = jnp.sum(parts_ref[...], axis=0)
    gate = summed[:, :width]
    up = summed[:, width : 2 * width]
    hidden_grad = summed[:, 2 * width :]
    sigma = 1.0 / (1.0 + jnp.exp(-gate))
    active = gate * sigma
    out_ref[:, :width] = (active * up).astype(BF16)
    out_ref[:, width : 2 * width] = (hidden_grad * up * sigma * (1.0 + gate * (1.0 - sigma))).astype(BF16)
    out_ref[:, 2 * width :] = (hidden_grad * active).astype(BF16)


def input_grads(triple_ref, gate_ref, up_ref, out_ref):
    tokens = triple_ref.shape[0]
    width = gate_ref.shape[1]
    depth = gate_ref.shape[0]
    both = triple_ref[:, width:]
    step = 256
    top = upper((tokens // 8, 8, step))
    for n in range(0, depth // 2, step):
        sides = []
        for at in (n, depth // 2 + n):
            joined = jnp.concatenate([gate_ref[at : at + step, :], up_ref[at : at + step, :]], axis=1)
            product = lax.dot_general(both, joined, LAST, preferred_element_type=F32)
            sides.append(product.reshape(tokens // 8, 8, step))
        left, right = sides
        out_ref[:, 0, :, n : n + step] = jnp.where(top, left, pltpu.roll(right, 4, 1)).astype(BF16)
        out_ref[:, 1, :, n : n + step] = jnp.where(top, pltpu.roll(left, 4, 1), right).astype(BF16)


def add_pieces(pieces_ref, out_ref):
    half = pieces_ref.shape[2]
    total = jnp.sum(pieces_ref[...].astype(F32), axis=0)
    out_ref[:, :half] = total[:4].astype(BF16)
    out_ref[:, half:] = pltpu.roll(total, 4, 0)[:4].astype(BF16)


def body(inputs, cotangent, gate_weight, up_weight, down_weight):
    own, depth = inputs.shape
    width = gate_weight.shape[1]
    columns = lax.axis_size("col")
    planes = lax.axis_size(DP)
    groups = columns * planes
    tokens = own * groups
    rows = 2 * columns * own
    shape = jax.ShapeDtypeStruct

    line = spread(jnp.concatenate([inputs, cotangent], axis=0), "col").reshape(columns, 2 * own, depth)
    copies = call(
        split_line,
        shape((planes, rows, depth), BF16),
        (0, planes * rows * depth * 2),
        out_specs=pl.BlockSpec(memory_space=pltpu.HBM),
        scratch_shapes=[pltpu.VMEM((rows, depth), BF16), pltpu.SemaphoreType.DMA((planes,))],
    )(line)
    plane = exchange(copies, DP).reshape(planes, rows, depth)

    core = lax.axis_index("core").astype(jnp.int32).reshape(1)
    other = run_forward(1 - core, plane, gate_weight, up_weight, down_weight)
    swapped = lax.ppermute(other, "core", [(0, 1), (1, 0)])
    mine = run_forward(core, plane, gate_weight, up_weight, down_weight)
    pair = mine + swapped

    pair, later = lax.optimization_barrier((pair, plane))
    parts = spread(pair, "z_hi").reshape(lax.axis_size("z_hi"), tokens // 2, 3 * width)
    gathered_in = later[:, : rows // 2].reshape(tokens, depth)
    gathered_cot = later[:, rows // 2 :].reshape(tokens, depth)
    parts, gathered_in, gathered_cot = lax.optimization_barrier((parts, gathered_in, gathered_cot))

    triple = call(activate, shape((tokens // 2, 3 * width), BF16), (tokens * width * 10, parts.size * 4))(parts)
    triple = lax.all_gather(triple, "core", axis=0, tiled=True)

    partial_in = call(
        input_grads,
        shape((groups // 2, 2, 2 * own, depth // 2), BF16),
        (4 * tokens * depth * width, 2 * tokens * depth + 4 * depth * width),
    )(triple, gate_weight, up_weight)
    pieces = exchange(partial_in.reshape(groups, 2 * own, depth // 2), GROUP)
    grad_inputs = call(add_pieces, shape((own, depth), BF16), (tokens * depth, 2 * tokens * depth))(pieces)

    hidden, gate_grad, up_grad = (triple[:, i * width : (i + 1) * width] for i in range(3))
    product = functools.partial(lax.dot_general, dimension_numbers=FIRST, preferred_element_type=F32)
    grad_gate_weight = product(gathered_in, gate_grad).astype(BF16)
    grad_up_weight = product(gathered_in, up_grad).astype(BF16)
    grad_down_weight = product(hidden, gathered_cot).astype(BF16)
    return (grad_inputs, grad_gate_weight, grad_up_weight, grad_down_weight)


def solution(mesh):
    fine = Mesh(mesh.devices.reshape(2, 4, 4, 2, 8), ("z_lo", "x", "z_hi", "core", "col"))
    in_specs = (P(GROUP, ROW), P(GROUP, ROW), P(ROW, GROUP), P(ROW, GROUP), P(GROUP, ROW))
    out_specs = (P(GROUP, ROW), P(ROW, GROUP), P(ROW, GROUP), P(GROUP, ROW))
    return jax.shard_map(body, mesh=fine, in_specs=in_specs, out_specs=out_specs, check_vma=False)
```

time: 141 us -> 132 us (0.936)
  blocking collectives: 50.3 us -> 19.7 us
  waiting for transfers between devices: 48 us -> 66.1 us
  starting transfers between devices: 17.2 us -> 31.3 us
  local copies, waits for them, and re-layouts: 10.3 us -> 4.8 us
  matrix products: 8.58 us -> 3.69 us
  Pallas kernels: 0 us -> 4.57 us
  other arithmetic: 4.83 us -> 0.78 us
    all_to_all x2 -> x1, blocking collectives: 48.3 us -> 17.8 us  [exchange(): return lax.all_to_all(pieces, axes, split_axis=0, concat_axis=0, tiled=True)]
    all_to_all x2 -> x3, waiting for transfers between devices: 46.6 us -> 65.1 us  [exchange(): return lax.all_to_all(pieces, axes, split_axis=0, concat_axis=0, tiled=True)]
    all_to_all x2 -> x3, starting transfers between devices: 15.3 us -> 29.3 us  [exchange(): return lax.all_to_all(pieces, axes, split_axis=0, concat_axis=0, tiled=True)]
    dot_general x6 -> x3, matrix products: 8.58 us -> 3.69 us  [the longest x1 1.28 us: body(): grad_up_weight = product(gathered_in, up_grad).astype(BF16)]
    pallas_call x0 -> x6, Pallas kernels: none -> 4.57 us  [the longest x1 1.44 us: body(): call(input_grads, shape((groups // 2, 2, 2 * own, depth // 2), BF16), (4...]
    reduce_sum x2 -> x0, other arithmetic: 2.99 us -> none  [the longest x1 2.28 us: body(): jnp.sum(pieces.astype(jnp.float32), axis=0).astype(jnp.bfloat16)]
    reshape x2 -> x0, local copies, waits for them, and re-layouts: 2.41 us -> none  [the longest x1 2.25 us: body(): pieces = exchange(partial_in.reshape(groups, own, depth), GROUP)]
    concatenate x1 -> x0, local copies, waits for them, and re-layouts: 1.9 us -> none  [body(): joined = jnp.concatenate([gate_weight, up_weight], axis=1)]
  transfers between devices with their start and end apart: 3 -> 4, of which waited for: 3 -> 4; matrix products, arithmetic and copies ran while one was open for 5% -> 4% of each run, Pallas kernels for 0% -> 0%
where the time goes in v3:
time: 132 us
  waiting for transfers between devices  66.1 us (50%)
  starting transfers between devices  31.3 us (24%)
  blocking collectives  19.7 us (15%)
  local copies, waits for them, and re-layouts  4.8 us (4%)
  Pallas kernels  4.57 us (3%)
  matrix products  3.69 us (3%)
    all_to_all x3, waiting for transfers between devices, exchange(): return lax.all_to_all(pieces, axes, split_axis=0, concat_axis=0, tiled=True)  65.1 us
    all_to_all x3, starting transfers between devices, exchange(): return lax.all_to_all(pieces, axes, split_axis=0, concat_axis=0, tiled=True)  29.3 us
    all_to_all x1, blocking collectives, exchange(): return lax.all_to_all(pieces, axes, split_axis=0, concat_axis=0, tiled=True)  17.8 us
  transfers between devices with their start and end apart: 4, of which 4 were waited for; matrix products, arithmetic and copies ran while one was open for 4% of the time, Pallas kernels for 0%

profile of v3, /device:TPU:8, one launch (start us, length us, event | category | flops | bytes accessed | tf_op | source)
XLA Modules:
  0.0 131.6 jit_solution(15099228222592823752)
XLA Ops:
  0.6 0.8 pad_maximum_fusion
  1.4 17.8 %all_to_all.20.line_ref = bf16[8,8,2048]{2,1,0:T(8,128)(2,1)S(1)} all-to-all(bf16[8,8,2048]{2,1,0:T(8,128)(2,1)S(1)} %broadcast_in_dim.4), channel_id=1, replica_groups=mesh['z_lo'=2,'x'=4,'z_hi'=4,'core'=2,'col'=8] {'col'}, dimensions={0} | all-to-all | bytes 524288 | tf_op jit(solution)/shard_map/all_to_all | solution.py:22
  19.2 0.3 shard_map.84
  19.5 0.0 copy-start
  19.5 1.3 %copy-done = bf16[8,64,2048]{2,1,0:T(8,128)(2,1)} copy-done((bf16[8,64,2048]{2,1,0:T(8,128)(2,1)}, bf16[8,64,2048]{2,1,0:T(8,128)(2,1)S(1)}, u32[]{:S(2)}) %copy-start) | copy-done | bytes 2097176
  20.8 0.0 copy-start.1
  20.8 0.0 copy-start.2
  20.8 6.2 %all-to-all-start.1 = ((bf16[8,64,2048]{2,1,0:T(8,128)(2,1)}), bf16[8,64,2048]{2,1,0:T(8,128)(2,1)S(1)}, u32[]{:S(2)}, u32[]{:S(2)}) async-start(bf16[8,64,2048]{2,1,0:T(8,128)(2,1)} %copy-done), calls=%async_computation.1 | async-start | bytes 4194304 | tf_op jit(solution)/shard_map/all_to_all | solution.py:22
  27.1 23.5 %all-to-all-done.1.plane_ref = bf16[8,64,2048]{2,1,0:T(8,128)(2,1)S(1)} async-done(((bf16[8,64,2048]{2,1,0:T(8,128)(2,1)}), bf16[8,64,2048]{2,1,0:T(8,128)(2,1)S(1)}, u32[]{:S(2)}, u32[]{:S(2)}) %all-to-all-start.1) | async-done | bytes 2097184 | tf_op jit(solution)/shard_map/all_to_all | solution.py:22
  50.5 0.0 copy-done.1
  50.5 0.0 copy-done.2
  50.5 0.0 copy-start.3
  50.5 1.0 copy-done.3
  51.6 0.4 shard_map.86
  52.0 1.9 %collective-permute-start = (f32[128,384]{1,0:T(8,128)S(1)}, f32[128,384]{1,0:T(8,128)S(1)}, u32[]{:S(2)}, u32[]{:S(2)}) collective-permute-start(f32[128,384]{1,0:T(8,128)S(1)} %shard_map.86), channel_id=1, source_target_pairs={{0,8},{8,0},{1,9},{9,1},{2,10},{10,2},{3,11},{11,3},{4,12},{12,4},... | collective-permute-start | bytes 589832 | tf_op jit(solution)/shard_map/ppermute | solution.py:156
  54.0 0.4 shard_map.85
  54.4 1.0 collective-permute-done
  55.4 0.9 broadcast_in_dim.5
  56.3 9.4 %all-to-all-start.2 = ((f32[4,128,384]{2,1,0:T(8,128)}), f32[4,128,384]{2,1,0:T(8,128)}, u32[]{:S(2)}, u32[]{:S(2)}) async-start(f32[4,128,384]{2,1,0:T(8,128)} %broadcast_in_dim.5), calls=%async_computation.2 | async-start | bytes 1572864 | tf_op jit(solution)/shard_map/all_to_all | solution.py:22
  65.7 1.5 %fusion.3 = (bf16[8,32,2048]{2,1,0:T(8,128)(2,1)}, bf16[8,32,2048]{2,1,0:T(8,128)(2,1)}) fusion(bf16[8,64,2048]{2,1,0:T(8,128)(2,1)S(1)} %all-to-all-done.1.plane_ref), kind=kLoop, calls=%fused_computation.7 | loop fusion | bytes 4194304 | tf_op jit(solution)/shard_map/slice | solution.py:163
  67.2 15.7 %all-to-all-done.2.parts_ref = f32[4,128,384]{2,1,0:T(8,128)} async-done(((f32[4,128,384]{2,1,0:T(8,128)}), f32[4,128,384]{2,1,0:T(8,128)}, u32[]{:S(2)}, u32[]{:S(2)}) %all-to-all-start.2) | async-done | bytes 786464 | tf_op jit(solution)/shard_map/all_to_all | solution.py:22
  82.9 1.2 shard_map.87
  84.1 1.9 %all_gather.3.triple_ref = bf16[256,384]{1,0:T(8,128)(2,1)S(1)} all-gather(bf16[128,384]{1,0:T(8,128)(2,1)S(1)} %shard_map.87), channel_id=1, replica_groups=mesh['z_lo'=2,'x'=4,'z_hi'=4,'core'=2,'col'=8] {'core'}, dimensions={0}, use_global_device_ids=true | all-gather | bytes 294912 | tf_op jit(solution)/shard_map/all_gather | solution.py:167
  86.0 1.4 %shard_map.88 = bf16[32,2,8,1024]{3,2,1,0:T(8,128)(2,1)} custom-call(bf16[256,384]{1,0:T(8,128)(2,1)S(1)} %all_gather.3.triple_ref, bf16[2048,128]{1,0:T(8,128)(2,1)S(1)} %copy-done.1, bf16[2048,128]{1,0:T(8,128)(2,1)S(1)} %copy-done.2), custom_call_target="tpu_custom_call" | custom-call | flops 268435456 | bytes 2097152 | tf_op jit(solution)/shard_map/pallas_call | solution.py:169
  87.5 0.0 copy-start.4
  87.5 13.7 %all-to-all-start.3 = ((bf16[64,8,1024]{2,1,0:T(8,128)(2,1)}), bf16[64,8,1024]{2,1,0:T(8,128)(2,1)S(1)}, u32[]{:S(2)}, u32[]{:S(2)}) async-start(bf16[64,8,1024]{2,1,0:T(8,128)(2,1)} %bitcast.3), calls=%async_computation.3 | async-start | bytes 2097152 | tf_op jit(solution)/shard_map/all_to_all | solution.py:22
  101.2 0.0 copy-done.4
  101.2 0.0 copy-start.5
  101.2 1.3 convolution_convert_fusion.1
  102.5 1.3 convolution_convert_fusion.2
  103.8 0.0 copy-done.5
  103.8 1.1 convolution_convert_fusion
  104.9 25.9 %all-to-all-done.3.pieces_ref = bf16[64,8,1024]{2,1,0:T(8,128)(2,1)S(1)} async-done(((bf16[64,8,1024]{2,1,0:T(8,128)(2,1)}), bf16[64,8,1024]{2,1,0:T(8,128)(2,1)S(1)}, u32[]{:S(2)}, u32[]{:S(2)}) %all-to-all-start.3) | async-done | bytes 1048608 | tf_op jit(solution)/shard_map/all_to_all | solution.py:22
  130.8 0.7 shard_map.89
  (2 shorter events, 0.0 us)
Async XLA Ops:
  19.5 1.3 %copy-start = (bf16[8,64,2048]{2,1,0:T(8,128)(2,1)}, bf16[8,64,2048]{2,1,0:T(8,128)(2,1)S(1)}, u32[]{:S(2)}) copy-start(bf16[8,64,2048]{2,1,0:T(8,128)(2,1)S(1)} %shard_map.84) | copy-start | bytes 6291460
  20.8 29.7 %copy-start.1 = (bf16[2048,128]{1,0:T(8,128)(2,1)S(1)}, bf16[2048,128]{1,0:T(8,128)(2,1)}, u32[]{:S(2)}) copy-start(bf16[2048,128]{1,0:T(8,128)(2,1)} %gate_ref.5) | copy-start | bytes 1572868
  20.8 29.7 %copy-start.2 = (bf16[2048,128]{1,0:T(8,128)(2,1)S(1)}, bf16[2048,128]{1,0:T(8,128)(2,1)}, u32[]{:S(2)}) copy-start(bf16[2048,128]{1,0:T(8,128)(2,1)} %up_ref.5) | copy-start | bytes 1572868
  20.8 29.7 %all-to-all-start.1 = ((bf16[8,64,2048]{2,1,0:T(8,128)(2,1)}), bf16[8,64,2048]{2,1,0:T(8,128)(2,1)S(1)}, u32[]{:S(2)}, u32[]{:S(2)}) async-start(bf16[8,64,2048]{2,1,0:T(8,128)(2,1)} %copy-done), calls=%async_computation.1 | async-start | bytes 4194304 | tf_op jit(solution)/shard_map/all_to_all | solution.py:22
  50.5 1.0 copy-start.3
  52.0 3.3 %collective-permute-start = (f32[128,384]{1,0:T(8,128)S(1)}, f32[128,384]{1,0:T(8,128)S(1)}, u32[]{:S(2)}, u32[]{:S(2)}) collective-permute-start(f32[128,384]{1,0:T(8,128)S(1)} %shard_map.86), channel_id=1, source_target_pairs={{0,8},{8,0},{1,9},{9,1},{2,10},{10,2},{3,11},{11,3},{4,12},{12,4},... | collective-permute-start | bytes 589832 | tf_op jit(solution)/shard_map/ppermute | solution.py:156
  56.3 26.6 %all-to-all-start.2 = ((f32[4,128,384]{2,1,0:T(8,128)}), f32[4,128,384]{2,1,0:T(8,128)}, u32[]{:S(2)}, u32[]{:S(2)}) async-start(f32[4,128,384]{2,1,0:T(8,128)} %broadcast_in_dim.5), calls=%async_computation.2 | async-start | bytes 1572864 | tf_op jit(solution)/shard_map/all_to_all | solution.py:22
  87.5 13.7 %copy-start.4 = (bf16[8,32,2048]{2,1,0:T(8,128)(2,1)S(1)}, bf16[8,32,2048]{2,1,0:T(8,128)(2,1)}, u32[]{:S(2)}) copy-start(bf16[8,32,2048]{2,1,0:T(8,128)(2,1)} %get-tuple-element.15) | copy-start | bytes 3145732
  87.5 43.4 %all-to-all-start.3 = ((bf16[64,8,1024]{2,1,0:T(8,128)(2,1)}), bf16[64,8,1024]{2,1,0:T(8,128)(2,1)S(1)}, u32[]{:S(2)}, u32[]{:S(2)}) async-start(bf16[64,8,1024]{2,1,0:T(8,128)(2,1)} %bitcast.3), calls=%async_computation.3 | async-start | bytes 2097152 | tf_op jit(solution)/shard_map/all_to_all | solution.py:22
  101.2 2.6 %copy-start.5 = (bf16[8,32,2048]{2,1,0:T(8,128)(2,1)S(1)}, bf16[8,32,2048]{2,1,0:T(8,128)(2,1)}, u32[]{:S(2)}) copy-start(bf16[8,32,2048]{2,1,0:T(8,128)(2,1)} %get-tuple-element.14) | copy-start | bytes 3145732

commit v4 on v3

--- a/solution.py
+++ b/solution.py
@@ -11,7 +11,10 @@
 DP = ("z_lo", "x")
 GROUP = ("z_lo", "x", "col")
 ROW = ("z_hi", "core")
-LIMIT = 40 * 1024 * 1024
+MIB = 1024 * 1024
+EXTRA = 16
+TOP = 14
+F16 = jnp.float16
 F32 = jnp.float32
 BF16 = jnp.bfloat16
 LAST = (((1,), (1,)), ((), ()))
@@ -27,13 +30,13 @@
     return exchange(jnp.broadcast_to(block[None], (n,) + block.shape), axes)
 
 
-def call(kernel, out_shape, cost, **rest):
+def call(kernel, out_shape, cost, limit=20, **rest):
     flops, size = cost
     return pl.pallas_call(
         kernel,
         out_shape=out_shape,
         cost_estimate=pl.CostEstimate(flops=flops, bytes_accessed=size, transcendentals=0),
-        compiler_params=pltpu.CompilerParams(vmem_limit_bytes=LIMIT),
+        compiler_params=pltpu.CompilerParams(vmem_limit_bytes=limit * MIB),
         **rest,
     )
 
@@ -93,9 +96,22 @@
     )(which, plane, gate_weight, up_weight, down_weight)
 
 
+def scale_pair(mine_ref, swapped_ref, out_ref):
+    tokens = mine_ref.shape[0]
+    pair = mine_ref[...] + swapped_ref[...]
+    largest = jnp.max(jnp.abs(pair), axis=0, keepdims=True)
+    power = jnp.floor(jnp.log2(jnp.maximum(largest, 1e-30)))
+    out_ref[:tokens, :] = pair * jnp.exp2(-power) * 2.0**TOP
+    out_ref[tokens:, :] = jnp.broadcast_to(power, (EXTRA, pair.shape[1]))
+
+
 def activate(parts_ref, out_ref):
+    tokens = out_ref.shape[0]
     width = out_ref.shape[1] // 3
-    summed = jnp.sum(parts_ref[...], axis=0)
+    summed = 0.0
+    for z in range(parts_ref.shape[0]):
+        power = parts_ref[z, tokens:, :][:1]
+        summed = summed + parts_ref[z, :tokens, :] * (jnp.exp2(power) * 2.0**-TOP)
     gate = summed[:, :width]
     up = summed[:, width : 2 * width]
     hidden_grad = summed[:, 2 * width :]
@@ -146,6 +162,7 @@
         split_line,
         shape((planes, rows, depth), BF16),
         (0, planes * rows * depth * 2),
+        limit=60,
         out_specs=pl.BlockSpec(memory_space=pltpu.HBM),
         scratch_shapes=[pltpu.VMEM((rows, depth), BF16), pltpu.SemaphoreType.DMA((planes,))],
     )(line)
@@ -155,15 +172,18 @@
     other = run_forward(1 - core, plane, gate_weight, up_weight, down_weight)
     swapped = lax.ppermute(other, "core", [(0, 1), (1, 0)])
     mine = run_forward(core, plane, gate_weight, up_weight, down_weight)
-    pair = mine + swapped
-
-    pair, later = lax.optimization_barrier((pair, plane))
-    parts = spread(pair, "z_hi").reshape(lax.axis_size("z_hi"), tokens // 2, 3 * width)
+    scaled = call(
+        scale_pair,
+        shape((tokens // 2 + EXTRA, 3 * width), F32),
+        (tokens * width * 10, tokens * width * 18),
+    )(mine, swapped).astype(F16)
+    scaled, later = lax.optimization_barrier((scaled, plane))
+    parts = spread(scaled, "z_hi").reshape((lax.axis_size("z_hi"),) + scaled.shape)
     gathered_in = later[:, : rows // 2].reshape(tokens, depth)
     gathered_cot = later[:, rows // 2 :].reshape(tokens, depth)
     parts, gathered_in, gathered_cot = lax.optimization_barrier((parts, gathered_in, gathered_cot))
 
-    triple = call(activate, shape((tokens // 2, 3 * width), BF16), (tokens * width * 10, parts.size * 4))(parts)
+    triple = call(activate, shape((tokens // 2, 3 * width), BF16), (tokens * width * 10, parts.size * 4))(parts.astype(F32))
     triple = lax.all_gather(triple, "core", axis=0, tiled=True)
 
     partial_in = call(

time: 132 us -> 126 us (0.955)
  starting transfers between devices: 31.3 us -> 27.2 us
  waiting for transfers between devices: 66.1 us -> 62.6 us
  local copies, waits for them, and re-layouts: 4.8 us -> 3.35 us
    all_to_all x3, starting transfers between devices: 29.3 us -> 25.3 us  [exchange(): return lax.all_to_all(pieces, axes, split_axis=0, concat_axis=0, tiled=True)]
    all_to_all x3, waiting for transfers between devices: 65.1 us -> 61.7 us  [exchange(): return lax.all_to_all(pieces, axes, split_axis=0, concat_axis=0, tiled=True)]
    pallas_call x1, Pallas kernels: 0.31 us -> 2.42 us  [body(): call(split_line, shape((planes, rows, depth), BF16), (0, planes * rows *...]
where the time goes in v4:
time: 126 us; the launch traced here: 125 us
  waiting for transfers between devices  62.6 us (50%)
  starting transfers between devices  27.2 us (22%)
  blocking collectives  19.9 us (16%)
  Pallas kernels  5.64 us (4%)
  matrix products  3.69 us (3%)
  local copies, waits for them, and re-layouts  3.35 us (3%)
  other arithmetic  1.85 us (1%)
    all_to_all x3, waiting for transfers between devices, exchange(): return lax.all_to_all(pieces, axes, split_axis=0, concat_axis=0, tiled=True)  61.7 us
    all_to_all x3, starting transfers between devices, exchange(): return lax.all_to_all(pieces, axes, split_axis=0, concat_axis=0, tiled=True)  25.3 us
    all_to_all x1, blocking collectives, exchange(): return lax.all_to_all(pieces, axes, split_axis=0, concat_axis=0, tiled=True)  17.9 us
  transfers between devices with their start and end apart: 4, of which 4 were waited for; matrix products, arithmetic and copies ran while one was open for 4% of the time, Pallas kernels for 0%

profile of v4, /device:TPU:8, one launch (start us, length us, event | category | flops | bytes accessed | tf_op | source)
XLA Modules:
  0.0 125.0 jit_solution(11444814305930580223)
XLA Ops:
  0.6 0.8 pad_maximum_fusion
  1.4 17.9 %all_to_all.20.line_ref = bf16[8,8,2048]{2,1,0:T(8,128)(2,1)} all-to-all(bf16[8,8,2048]{2,1,0:T(8,128)(2,1)S(1)} %broadcast_in_dim.4), channel_id=1, replica_groups=mesh['z_lo'=2,'x'=4,'z_hi'=4,'core'=2,'col'=8] {'col'}, dimensions={0} | all-to-all | bytes 524288 | tf_op jit(solution)/shard_map/all_to_all | solution.py:25
  19.3 2.4 %shard_map.84 = bf16[8,64,2048]{2,1,0:T(8,128)(2,1)} custom-call(bf16[8,8,2048]{2,1,0:T(8,128)(2,1)} %all_to_all.20.line_ref), custom_call_target="tpu_custom_call" | custom-call | bytes 2097152 | tf_op jit(solution)/shard_map/pallas_call | solution.py:161
  21.8 0.0 copy-start
  21.8 0.0 copy-start.1
  21.8 6.2 %all-to-all-start.1 = ((bf16[8,64,2048]{2,1,0:T(8,128)(2,1)}), bf16[8,64,2048]{2,1,0:T(8,128)(2,1)S(1)}, u32[]{:S(2)}, u32[]{:S(2)}) async-start(bf16[8,64,2048]{2,1,0:T(8,128)(2,1)} %shard_map.84), calls=%async_computation.1 | async-start | bytes 4194304 | tf_op jit(solution)/shard_map/all_to_all | solution.py:25
  28.0 23.5 %all-to-all-done.1.plane_ref = bf16[8,64,2048]{2,1,0:T(8,128)(2,1)S(1)} async-done(((bf16[8,64,2048]{2,1,0:T(8,128)(2,1)}), bf16[8,64,2048]{2,1,0:T(8,128)(2,1)S(1)}, u32[]{:S(2)}, u32[]{:S(2)}) %all-to-all-start.1) | async-done | bytes 2097184 | tf_op jit(solution)/shard_map/all_to_all | solution.py:25
  51.5 0.0 copy-done
  51.5 0.0 copy-done.1
  51.5 0.0 copy-start.2
  51.5 1.0 copy-done.2
  52.5 0.0 copy-start.3
  52.5 0.4 shard_map.86
  53.0 1.9 %collective-permute-start = (f32[128,384]{1,0:T(8,128)S(1)}, f32[128,384]{1,0:T(8,128)S(1)}, u32[]{:S(2)}, u32[]{:S(2)}) collective-permute-start(f32[128,384]{1,0:T(8,128)S(1)} %shard_map.86), channel_id=1, source_target_pairs={{0,8},{8,0},{1,9},{9,1},{2,10},{10,2},{3,11},{11,3},{4,12},{12,4},... | collective-permute-start | bytes 589832 | tf_op jit(solution)/shard_map/ppermute | solution.py:173
  54.9 0.0 copy-done.3
  54.9 0.4 shard_map.85.mine_ref
  55.3 0.9 collective-permute-done.swapped_ref
  56.3 0.1 shard_map.87
  56.4 0.8 broadcast_in_dim.5
  57.2 9.4 %all-to-all-start.2 = ((f16[4,144,384]{2,1,0:T(8,128)(2,1)}), f16[4,144,384]{2,1,0:T(8,128)(2,1)}, u32[]{:S(2)}, u32[]{:S(2)}) async-start(f16[4,144,384]{2,1,0:T(8,128)(2,1)} %broadcast_in_dim.5), calls=%async_computation.2 | async-start | bytes 884736 | tf_op jit(solution)/shard_map/all_to_all | solution.py:25
  66.6 1.5 %fusion.3 = (bf16[8,32,2048]{2,1,0:T(8,128)(2,1)}, bf16[8,32,2048]{2,1,0:T(8,128)(2,1)}) fusion(bf16[8,64,2048]{2,1,0:T(8,128)(2,1)S(1)} %all-to-all-done.1.plane_ref), kind=kLoop, calls=%fused_computation.7 | loop fusion | bytes 4194304 | tf_op jit(solution)/shard_map/slice | solution.py:183
  68.0 12.3 %all-to-all-done.2 = f16[4,144,384]{2,1,0:T(8,128)(2,1)} async-done(((f16[4,144,384]{2,1,0:T(8,128)(2,1)}), f16[4,144,384]{2,1,0:T(8,128)(2,1)}, u32[]{:S(2)}, u32[]{:S(2)}) %all-to-all-start.2) | async-done | bytes 442400 | tf_op jit(solution)/shard_map/all_to_all | solution.py:25
  80.3 1.1 convert_element_type.16.parts_ref
  81.4 0.1 shard_map.88
  81.5 1.9 %all_gather.3.triple_ref = bf16[256,384]{1,0:T(8,128)(2,1)S(1)} all-gather(bf16[128,384]{1,0:T(8,128)(2,1)S(1)} %shard_map.88), channel_id=1, replica_groups=mesh['z_lo'=2,'x'=4,'z_hi'=4,'core'=2,'col'=8] {'core'}, dimensions={0}, use_global_device_ids=true | all-gather | bytes 294912 | tf_op jit(solution)/shard_map/all_gather | solution.py:187
  83.5 1.4 %shard_map.89 = bf16[32,2,8,1024]{3,2,1,0:T(8,128)(2,1)} custom-call(bf16[256,384]{1,0:T(8,128)(2,1)S(1)} %all_gather.3.triple_ref, bf16[2048,128]{1,0:T(8,128)(2,1)S(1)} %copy-done, bf16[2048,128]{1,0:T(8,128)(2,1)S(1)} %copy-done.1), custom_call_target="tpu_custom_call" | custom-call | flops 268435456 | bytes 2097152 | tf_op jit(solution)/shard_map/pallas_call | solution.py:189
  84.9 0.0 copy-start.4
  84.9 9.7 %all-to-all-start.3 = ((bf16[64,8,1024]{2,1,0:T(8,128)(2,1)}), bf16[64,8,1024]{2,1,0:T(8,128)(2,1)S(1)}, u32[]{:S(2)}, u32[]{:S(2)}) async-start(bf16[64,8,1024]{2,1,0:T(8,128)(2,1)} %bitcast.3), calls=%async_computation.3 | async-start | bytes 2097152 | tf_op jit(solution)/shard_map/all_to_all | solution.py:25
  94.6 0.0 copy-done.4
  94.6 0.0 copy-start.5
  94.6 1.3 %convolution_convert_fusion.1 = bf16[2048,128]{1,0:T(8,128)(2,1)} fusion(bf16[256,2048]{1,0:T(8,128)(2,1)S(1)} %bitcast.7, bf16[256,384]{1,0:T(8,128)(2,1)S(1)} %all_gather.3.triple_ref), kind=kOutput, calls=%fused_computation.1 | convolution fusion | flops 134479872 | bytes 1638400 | tf_op jit(solution)/shard_map/dot_general | solution.py:200
  95.9 1.3 %convolution_convert_fusion.2 = bf16[2048,128]{1,0:T(8,128)(2,1)} fusion(bf16[256,2048]{1,0:T(8,128)(2,1)S(1)} %bitcast.8, bf16[256,384]{1,0:T(8,128)(2,1)S(1)} %all_gather.3.triple_ref), kind=kOutput, calls=%fused_computation.2 | convolution fusion | flops 134479872 | bytes 1638400 | tf_op jit(solution)/shard_map/dot_general | solution.py:199
  97.2 0.0 copy-done.5
  97.2 1.1 convolution_convert_fusion
  98.3 25.9 %all-to-all-done.3.pieces_ref = bf16[64,8,1024]{2,1,0:T(8,128)(2,1)S(1)} async-done(((bf16[64,8,1024]{2,1,0:T(8,128)(2,1)}), bf16[64,8,1024]{2,1,0:T(8,128)(2,1)S(1)}, u32[]{:S(2)}, u32[]{:S(2)}) %all-to-all-start.3) | async-done | bytes 1048608 | tf_op jit(solution)/shard_map/all_to_all | solution.py:25
  124.2 0.7 shard_map.90
  (2 shorter events, 0.0 us)
Async XLA Ops:
  21.8 29.7 %copy-start = (bf16[2048,128]{1,0:T(8,128)(2,1)S(1)}, bf16[2048,128]{1,0:T(8,128)(2,1)}, u32[]{:S(2)}) copy-start(bf16[2048,128]{1,0:T(8,128)(2,1)} %gate_ref.5) | copy-start | bytes 1572868
  21.8 29.7 %copy-start.1 = (bf16[2048,128]{1,0:T(8,128)(2,1)S(1)}, bf16[2048,128]{1,0:T(8,128)(2,1)}, u32[]{:S(2)}) copy-start(bf16[2048,128]{1,0:T(8,128)(2,1)} %up_ref.5) | copy-start | bytes 1572868
  21.8 29.7 %all-to-all-start.1 = ((bf16[8,64,2048]{2,1,0:T(8,128)(2,1)}), bf16[8,64,2048]{2,1,0:T(8,128)(2,1)S(1)}, u32[]{:S(2)}, u32[]{:S(2)}) async-start(bf16[8,64,2048]{2,1,0:T(8,128)(2,1)} %shard_map.84), calls=%async_computation.1 | async-start | bytes 4194304 | tf_op jit(solution)/shard_map/all_to_all | solution.py:25
  51.5 1.0 copy-start.2
  52.5 2.4 %copy-start.3 = (bf16[128,2048]{1,0:T(8,128)(2,1)S(1)}, bf16[128,2048]{1,0:T(8,128)(2,1)}, u32[]{:S(2)}) copy-start(bf16[128,2048]{1,0:T(8,128)(2,1)} %down_ref.3) | copy-start | bytes 1572868
  53.0 3.3 %collective-permute-start = (f32[128,384]{1,0:T(8,128)S(1)}, f32[128,384]{1,0:T(8,128)S(1)}, u32[]{:S(2)}, u32[]{:S(2)}) collective-permute-start(f32[128,384]{1,0:T(8,128)S(1)} %shard_map.86), channel_id=1, source_target_pairs={{0,8},{8,0},{1,9},{9,1},{2,10},{10,2},{3,11},{11,3},{4,12},{12,4},... | collective-permute-start | bytes 589832 | tf_op jit(solution)/shard_map/ppermute | solution.py:173
  57.2 23.1 %all-to-all-start.2 = ((f16[4,144,384]{2,1,0:T(8,128)(2,1)}), f16[4,144,384]{2,1,0:T(8,128)(2,1)}, u32[]{:S(2)}, u32[]{:S(2)}) async-start(f16[4,144,384]{2,1,0:T(8,128)(2,1)} %broadcast_in_dim.5), calls=%async_computation.2 | async-start | bytes 884736 | tf_op jit(solution)/shard_map/all_to_all | solution.py:25
  84.9 9.7 %copy-start.4 = (bf16[8,32,2048]{2,1,0:T(8,128)(2,1)S(1)}, bf16[8,32,2048]{2,1,0:T(8,128)(2,1)}, u32[]{:S(2)}) copy-start(bf16[8,32,2048]{2,1,0:T(8,128)(2,1)} %get-tuple-element.15) | copy-start | bytes 3145732
  84.9 39.3 %all-to-all-start.3 = ((bf16[64,8,1024]{2,1,0:T(8,128)(2,1)}), bf16[64,8,1024]{2,1,0:T(8,128)(2,1)S(1)}, u32[]{:S(2)}, u32[]{:S(2)}) async-start(bf16[64,8,1024]{2,1,0:T(8,128)(2,1)} %bitcast.3), calls=%async_computation.3 | async-start | bytes 2097152 | tf_op jit(solution)/shard_map/all_to_all | solution.py:25
  94.6 2.6 %copy-start.5 = (bf16[8,32,2048]{2,1,0:T(8,128)(2,1)S(1)}, bf16[8,32,2048]{2,1,0:T(8,128)(2,1)}, u32[]{:S(2)}) copy-start(bf16[8,32,2048]{2,1,0:T(8,128)(2,1)} %get-tuple-element.14) | copy-start | bytes 3145732

commit v5 on v4

--- a/solution.py
+++ b/solution.py
@@ -1,5 +1,3 @@
-import functools
-
 import jax
 import jax.numpy as jnp
 from jax import lax
@@ -124,20 +122,39 @@
 
 def input_grads(triple_ref, gate_ref, up_ref, out_ref):
     tokens = triple_ref.shape[0]
-    width = gate_ref.shape[1]
-    depth = gate_ref.shape[0]
+    depth, width = gate_ref.shape
     both = triple_ref[:, width:]
     step = 256
-    top = upper((tokens // 8, 8, step))
-    for n in range(0, depth // 2, step):
-        sides = []
-        for at in (n, depth // 2 + n):
-            joined = jnp.concatenate([gate_ref[at : at + step, :], up_ref[at : at + step, :]], axis=1)
-            product = lax.dot_general(both, joined, LAST, preferred_element_type=F32)
-            sides.append(product.reshape(tokens // 8, 8, step))
-        left, right = sides
-        out_ref[:, 0, :, n : n + step] = jnp.where(top, left, pltpu.roll(right, 4, 1)).astype(BF16)
-        out_ref[:, 1, :, n : n + step] = jnp.where(top, pltpu.roll(left, 4, 1), right).astype(BF16)
+    for n in range(0, depth, step):
+        joined = jnp.concatenate([gate_ref[n : n + step, :], up_ref[n : n + step, :]], axis=1)
+        product = lax.dot_general(both, joined, LAST, preferred_element_type=F32)
+        out_ref[:, :, n : n + step] = product.reshape(out_ref.shape[:2] + (step,)).astype(BF16)
+
+
+def add_planes(pieces_ref, out_ref):
+    _, rows, depth = pieces_ref.shape
+    half = depth // 2
+    total = pieces_ref[0].astype(F32)
+    for p in range(1, pieces_ref.shape[0]):
+        total = total + pieces_ref[p].astype(F32)
+    left = total[:, :half].reshape(rows // 8, 8, half)
+    right = total[:, half:].reshape(rows // 8, 8, half)
+    top = upper(left.shape)
+    out_ref[:, 0] = jnp.where(top, left, pltpu.roll(right, 4, 1)).astype(BF16)
+    out_ref[:, 1] = jnp.where(top, pltpu.roll(left, 4, 1), right).astype(BF16)
+
+
+def weight_grads(triple_ref, plane_ref, gate_ref, up_ref, down_ref):
+    planes, rows, step = plane_ref.shape
+    half = rows // 2
+    width = gate_ref.shape[1]
+    inputs = plane_ref[:, :half, :].reshape(planes * half, step)
+    cotangents = plane_ref[:, half:, :].reshape(planes * half, step)
+    both = lax.dot_general(inputs, triple_ref[:, width:], FIRST, preferred_element_type=F32)
+    gate_ref[...] = both[:, :width].astype(BF16)
+    up_ref[...] = both[:, width:].astype(BF16)
+    hidden = triple_ref[:, :width]
+    down_ref[...] = lax.dot_general(hidden, cotangents, FIRST, preferred_element_type=F32).astype(BF16)
 
 
 def add_pieces(pieces_ref, out_ref):
@@ -158,18 +175,18 @@
     shape = jax.ShapeDtypeStruct
 
     line = spread(jnp.concatenate([inputs, cotangent], axis=0), "col").reshape(columns, 2 * own, depth)
+    core = lax.axis_index("core").astype(jnp.int32).reshape(1)
+    line, core, flipped = lax.optimization_barrier((line, core, 1 - core))
     copies = call(
         split_line,
         shape((planes, rows, depth), BF16),
         (0, planes * rows * depth * 2),
-        limit=60,
-        out_specs=pl.BlockSpec(memory_space=pltpu.HBM),
+        out_specs=pl.BlockSpec(memory_space=pl.ANY),
         scratch_shapes=[pltpu.VMEM((rows, depth), BF16), pltpu.SemaphoreType.DMA((planes,))],
     )(line)
     plane = exchange(copies, DP).reshape(planes, rows, depth)
 
-    core = lax.axis_index("core").astype(jnp.int32).reshape(1)
-    other = run_forward(1 - core, plane, gate_weight, up_weight, down_weight)
+    other = run_forward(flipped, plane, gate_weight, up_weight, down_weight)
     swapped = lax.ppermute(other, "core", [(0, 1), (1, 0)])
     mine = run_forward(core, plane, gate_weight, up_weight, down_weight)
     scaled = call(
@@ -177,28 +194,40 @@
         shape((tokens // 2 + EXTRA, 3 * width), F32),
         (tokens * width * 10, tokens * width * 18),
     )(mine, swapped).astype(F16)
-    scaled, later = lax.optimization_barrier((scaled, plane))
     parts = spread(scaled, "z_hi").reshape((lax.axis_size("z_hi"),) + scaled.shape)
-    gathered_in = later[:, : rows // 2].reshape(tokens, depth)
-    gathered_cot = later[:, rows // 2 :].reshape(tokens, depth)
-    parts, gathered_in, gathered_cot = lax.optimization_barrier((parts, gathered_in, gathered_cot))
 
     triple = call(activate, shape((tokens // 2, 3 * width), BF16), (tokens * width * 10, parts.size * 4))(parts.astype(F32))
     triple = lax.all_gather(triple, "core", axis=0, tiled=True)
 
     partial_in = call(
         input_grads,
-        shape((groups // 2, 2, 2 * own, depth // 2), BF16),
+        shape((planes, columns * own, depth), BF16),
         (4 * tokens * depth * width, 2 * tokens * depth + 4 * depth * width),
     )(triple, gate_weight, up_weight)
-    pieces = exchange(partial_in.reshape(groups, 2 * own, depth // 2), GROUP)
-    grad_inputs = call(add_pieces, shape((own, depth), BF16), (tokens * depth, 2 * tokens * depth))(pieces)
-
-    hidden, gate_grad, up_grad = (triple[:, i * width : (i + 1) * width] for i in range(3))
-    product = functools.partial(lax.dot_general, dimension_numbers=FIRST, preferred_element_type=F32)
-    grad_gate_weight = product(gathered_in, gate_grad).astype(BF16)
-    grad_up_weight = product(gathered_in, up_grad).astype(BF16)
-    grad_down_weight = product(hidden, gathered_cot).astype(BF16)
+    line_in = call(
+        add_planes,
+        shape((columns // 2, 2, 2 * own, depth // 2), BF16),
+        (tokens * depth, 2 * tokens * depth),
+    )(exchange(partial_in, DP))
+    line_in, later = lax.optimization_barrier((line_in, triple))
+    pieces = exchange(line_in.reshape(columns, 2 * own, depth // 2), "col")
+    step = depth // 4
+    grad_gate_weight, grad_up_weight, grad_down_weight = call(
+        weight_grads,
+        [shape(w.shape, BF16) for w in (gate_weight, up_weight, down_weight)],
+        (6 * tokens * depth * width, plane.size * 2 + 6 * depth * width),
+        grid=(4,),
+        in_specs=[
+            pl.BlockSpec(triple.shape, lambda n: (0, 0)),
+            pl.BlockSpec((planes, rows, step), lambda n: (0, 0, n)),
+        ],
+        out_specs=[
+            pl.BlockSpec((step, width), lambda n: (n, 0)),
+            pl.BlockSpec((step, width), lambda n: (n, 0)),
+            pl.BlockSpec((width, step), lambda n: (0, n)),
+        ],
+    )(later, plane)
+    grad_inputs = call(add_pieces, shape((own, depth), BF16), (columns * own * depth, 2 * columns * own * depth))(pieces)
     return (grad_inputs, grad_gate_weight, grad_up_weight, grad_down_weight)
 
 

time: 126 us -> 116 us (0.921)
  blocking collectives: 19.9 us -> 75.3 us
  waiting for transfers between devices: 62.6 us -> 15.1 us
  starting transfers between devices: 27.2 us -> 16.4 us
  matrix products: 3.69 us -> 0 us
  local copies, waits for them, and re-layouts: 3.35 us -> 0.79 us
    all_to_all x1 -> x3, blocking collectives: 17.9 us -> 73.4 us  [exchange(): return lax.all_to_all(pieces, axes, split_axis=0, concat_axis=0, tiled=True)]
    all_to_all x3 -> x2, waiting for transfers between devices: 61.7 us -> 14.2 us  [exchange(): return lax.all_to_all(pieces, axes, split_axis=0, concat_axis=0, tiled=True)]
    all_to_all x3 -> x2, starting transfers between devices: 25.3 us -> 14.5 us  [exchange(): return lax.all_to_all(pieces, axes, split_axis=0, concat_axis=0, tiled=True)]
    dot_general x3 -> x0, matrix products: 3.69 us -> none  [the longest x1 1.28 us: body(): grad_up_weight = product(gathered_in, up_grad).astype(BF16)]
    pallas_call x2 -> x4, Pallas kernels: 2.19 us -> 4.44 us  [the longest x1 2.53 us: body(): call(weight_grads, [shape(w.shape, BF16) for w in (gate_weight, up_weight...]
    pallas_call x1, Pallas kernels: 2.42 us -> 0.31 us  [body(): call(split_line, shape((planes, rows, depth), BF16), (0, planes * rows *...]
    slice x1 -> x0, local copies, waits for them, and re-layouts: 1.46 us -> none  [body(): gathered_cot = later[:, rows // 2:].reshape(tokens, depth)]
  transfers between devices with their start and end apart: 4 -> 3, of which waited for: 4 -> 3; matrix products, arithmetic and copies ran while one was open for 4% -> 0% of each run, Pallas kernels for 0% -> 3%
where the time goes in v5:
time: 116 us; the launch traced here: 115 us
  blocking collectives  75.3 us (65%)
  starting transfers between devices  16.4 us (14%)
  waiting for transfers between devices  15.1 us (13%)
  Pallas kernels  5.83 us (5%)
    all_to_all x3, blocking collectives, exchange(): return lax.all_to_all(pieces, axes, split_axis=0, concat_axis=0, tiled=True)  73.4 us
    all_to_all x2, starting transfers between devices, exchange(): return lax.all_to_all(pieces, axes, split_axis=0, concat_axis=0, tiled=True)  14.5 us
    all_to_all x2, waiting for transfers between devices, exchange(): return lax.all_to_all(pieces, axes, split_axis=0, concat_axis=0, tiled=True)  14.2 us
    pallas_call x1, Pallas kernels, body(): call(weight_grads, [shape(w.shape, BF16) for w in (gate_weight, up_weight...  2.53 us
  transfers between devices with their start and end apart: 3, of which 3 were waited for; matrix products, arithmetic and copies ran while one was open for 0% of the time, Pallas kernels for 3%

profile of v5, /device:TPU:8, one launch (start us, length us, event | category | flops | bytes accessed | tf_op | source)
XLA Modules:
  0.0 115.1 jit_solution(4509579248229511971)
XLA Ops:
  0.6 0.8 pad_maximum_fusion
  1.4 0.7 broadcast_in_dim.4
  2.1 9.1 %all-to-all-start = ((bf16[8,8,2048]{2,1,0:T(8,128)(2,1)}), bf16[8,8,2048]{2,1,0:T(8,128)(2,1)S(1)}, u32[]{:S(2)}, u32[]{:S(2)}) async-start(bf16[8,8,2048]{2,1,0:T(8,128)(2,1)} %broadcast_in_dim.4), calls=%async_computation | async-start | bytes 524288 | tf_op jit(solution)/shard_map/all_to_all | solution.py:23
  11.2 9.1 %all-to-all-done.line_ref = bf16[8,8,2048]{2,1,0:T(8,128)(2,1)S(1)} async-done(((bf16[8,8,2048]{2,1,0:T(8,128)(2,1)}), bf16[8,8,2048]{2,1,0:T(8,128)(2,1)S(1)}, u32[]{:S(2)}, u32[]{:S(2)}) %all-to-all-start) | async-done | bytes 262176 | tf_op jit(solution)/shard_map/all_to_all | solution.py:23
  20.3 0.3 shard_map.84
  20.6 0.0 copy-start
  20.6 0.0 copy-start.1
  20.6 0.0 copy-start.2
  20.7 30.3 %all_to_all.25.plane_ref = bf16[8,64,2048]{2,1,0:T(8,128)(2,1)S(1)} all-to-all(bf16[8,64,2048]{2,1,0:T(8,128)(2,1)S(1)} %shard_map.84), channel_id=1, replica_groups=mesh['z_lo'=2,'x'=4,'z_hi'=4,'core'=2,'col'=8] {'z_lo','x'}, dimensions={0} | all-to-all | bytes 4194304 | tf_op jit(solution)/shard_map/all_to_all | solution.py:23
  51.0 0.0 copy-done
  51.0 0.0 copy-done.1
  51.0 0.0 copy-done.2
  51.0 0.5 shard_map.86
  51.5 1.9 %collective-permute-start = (f32[128,384]{1,0:T(8,128)S(1)}, f32[128,384]{1,0:T(8,128)S(1)}, u32[]{:S(2)}, u32[]{:S(2)}) collective-permute-start(f32[128,384]{1,0:T(8,128)S(1)} %shard_map.86), channel_id=1, source_target_pairs={{0,8},{8,0},{1,9},{9,1},{2,10},{10,2},{3,11},{11,3},{4,12},{12,4},... | collective-permute-start | bytes 589832 | tf_op jit(solution)/shard_map/ppermute | solution.py:190
  53.4 0.5 shard_map.85.mine_ref
  53.9 0.9 collective-permute-done.swapped_ref
  54.8 0.1 shard_map.87
  55.0 24.2 %all_to_all.26 = f16[4,144,384]{2,1,0:T(8,128)(2,1)S(1)} all-to-all(f16[4,144,384]{2,1,0:T(8,128)(2,1)S(1)} %broadcast_in_dim.5), channel_id=1, replica_groups=mesh['z_lo'=2,'x'=4,'z_hi'=4,'core'=2,'col'=8] {'z_hi'}, dimensions={0} | all-to-all | bytes 884736 | tf_op jit(solution)/shard_map/all_to_all | solution.py:23
  79.2 0.1 convert_element_type.7.parts_ref
  79.2 0.1 shard_map.88
  79.3 1.9 %all_gather.3.triple_ref = bf16[256,384]{1,0:T(8,128)(2,1)S(1)} all-gather(bf16[128,384]{1,0:T(8,128)(2,1)S(1)} %shard_map.88), channel_id=1, replica_groups=mesh['z_lo'=2,'x'=4,'z_hi'=4,'core'=2,'col'=8] {'core'}, dimensions={0}, use_global_device_ids=true | all-gather | bytes 294912 | tf_op jit(solution)/shard_map/all_gather | solution.py:200
  81.3 0.5 shard_map.89
  81.8 18.9 %all_to_all.27.pieces_ref = bf16[8,32,2048]{2,1,0:T(8,128)(2,1)S(1)} all-to-all(bf16[8,32,2048]{2,1,0:T(8,128)(2,1)S(1)} %shard_map.89), channel_id=1, replica_groups=mesh['z_lo'=2,'x'=4,'z_hi'=4,'core'=2,'col'=8] {'z_lo','x'}, dimensions={0} | all-to-all | bytes 2097152 | tf_op jit(solution)/shard_map/all_to_all | solution.py:23
  100.6 0.8 shard_map.90
  101.4 5.4 %all-to-all-start.4 = ((bf16[8,8,1024]{2,1,0:T(8,128)(2,1)}), bf16[8,8,1024]{2,1,0:T(8,128)(2,1)S(1)}, u32[]{:S(2)}, u32[]{:S(2)}) async-start(bf16[8,8,1024]{2,1,0:T(8,128)(2,1)} %bitcast.1), calls=%async_computation.4 | async-start | bytes 262144 | tf_op jit(solution)/shard_map/all_to_all | solution.py:23
  106.8 2.5 %shard_map.92 = (bf16[2048,128]{1,0:T(8,128)(2,1)}, bf16[2048,128]{1,0:T(8,128)(2,1)}, bf16[128,2048]{1,0:T(8,128)(2,1)}) custom-call(bf16[256,384]{1,0:T(8,128)(2,1)S(1)} %all_gather.3.triple_ref, bf16[8,64,2048]{2,1,0:T(8,128)(2,1)S(1)} %all_to_all.25.plane_ref), custom_call_target="tpu_custom_call" | custom-call | flops 402653184 | bytes 3670016 | tf_op jit(solution)/shard_map/pallas_call | solution.py:215
  109.3 5.1 %all-to-all-done.4.pieces_ref = bf16[8,8,1024]{2,1,0:T(8,128)(2,1)S(1)} async-done(((bf16[8,8,1024]{2,1,0:T(8,128)(2,1)}), bf16[8,8,1024]{2,1,0:T(8,128)(2,1)S(1)}, u32[]{:S(2)}, u32[]{:S(2)}) %all-to-all-start.4) | async-done | bytes 131104 | tf_op jit(solution)/shard_map/all_to_all | solution.py:23
  114.4 0.6 shard_map.91
  (2 shorter events, 0.1 us)
Async XLA Ops:
  2.1 18.2 %all-to-all-start = ((bf16[8,8,2048]{2,1,0:T(8,128)(2,1)}), bf16[8,8,2048]{2,1,0:T(8,128)(2,1)S(1)}, u32[]{:S(2)}, u32[]{:S(2)}) async-start(bf16[8,8,2048]{2,1,0:T(8,128)(2,1)} %broadcast_in_dim.4), calls=%async_computation | async-start | bytes 524288 | tf_op jit(solution)/shard_map/all_to_all | solution.py:23
  20.6 30.4 %copy-start = (bf16[2048,128]{1,0:T(8,128)(2,1)S(1)}, bf16[2048,128]{1,0:T(8,128)(2,1)}, u32[]{:S(2)}) copy-start(bf16[2048,128]{1,0:T(8,128)(2,1)} %gate_ref.5) | copy-start | bytes 1572868
  20.6 30.4 %copy-start.1 = (bf16[2048,128]{1,0:T(8,128)(2,1)S(1)}, bf16[2048,128]{1,0:T(8,128)(2,1)}, u32[]{:S(2)}) copy-start(bf16[2048,128]{1,0:T(8,128)(2,1)} %up_ref.5) | copy-start | bytes 1572868
  20.6 30.4 %copy-start.2 = (bf16[128,2048]{1,0:T(8,128)(2,1)S(1)}, bf16[128,2048]{1,0:T(8,128)(2,1)}, u32[]{:S(2)}) copy-start(bf16[128,2048]{1,0:T(8,128)(2,1)} %down_ref.3) | copy-start | bytes 1572868
  51.5 3.3 %collective-permute-start = (f32[128,384]{1,0:T(8,128)S(1)}, f32[128,384]{1,0:T(8,128)S(1)}, u32[]{:S(2)}, u32[]{:S(2)}) collective-permute-start(f32[128,384]{1,0:T(8,128)S(1)} %shard_map.86), channel_id=1, source_target_pairs={{0,8},{8,0},{1,9},{9,1},{2,10},{10,2},{3,11},{11,3},{4,12},{12,4},... | collective-permute-start | bytes 589832 | tf_op jit(solution)/shard_map/ppermute | solution.py:190
  101.4 13.0 %all-to-all-start.4 = ((bf16[8,8,1024]{2,1,0:T(8,128)(2,1)}), bf16[8,8,1024]{2,1,0:T(8,128)(2,1)S(1)}, u32[]{:S(2)}, u32[]{:S(2)}) async-start(bf16[8,8,1024]{2,1,0:T(8,128)(2,1)} %bitcast.1), calls=%async_computation.4 | async-start | bytes 262144 | tf_op jit(solution)/shard_map/all_to_all | solution.py:23

commit v6 on v5

--- a/solution.py
+++ b/solution.py
@@ -10,7 +10,7 @@
 GROUP = ("z_lo", "x", "col")
 ROW = ("z_hi", "core")
 MIB = 1024 * 1024
-EXTRA = 16
+EXTRA = 8
 TOP = 14
 F16 = jnp.float16
 F32 = jnp.float32
@@ -60,7 +60,7 @@
         copy.wait()
 
 
-def forward(which_ref, plane_ref, gate_ref, up_ref, down_ref, out_ref):
+def forward(plane_ref, gate_ref, up_ref, down_ref, out_ref):
     planes, rows, depth = plane_ref.shape
     half = rows // 2
     width = gate_ref.shape[1]
@@ -71,32 +71,9 @@
     out_ref[:, 2 * width :] = lax.dot_general(cotangents, down_ref[...], LAST, preferred_element_type=F32)
 
 
-def run_forward(which, plane, gate_weight, up_weight, down_weight):
-    planes, rows, depth = plane.shape
-    width = gate_weight.shape[1]
-    tokens = planes * rows // 4
-    whole = lambda i, c: (0, 0)
-    return call(
-        forward,
-        jax.ShapeDtypeStruct((tokens, 3 * width), F32),
-        (6 * tokens * depth * width, plane.size + 6 * depth * width),
-        grid_spec=pltpu.PrefetchScalarGridSpec(
-            num_scalar_prefetch=1,
-            grid=(1,),
-            in_specs=[
-                pl.BlockSpec((planes // 2, rows, depth), lambda i, c: (c[0], 0, 0)),
-                pl.BlockSpec(gate_weight.shape, whole),
-                pl.BlockSpec(up_weight.shape, whole),
-                pl.BlockSpec(down_weight.shape, whole),
-            ],
-            out_specs=pl.BlockSpec((tokens, 3 * width), whole),
-        ),
-    )(which, plane, gate_weight, up_weight, down_weight)
-
-
-def scale_pair(mine_ref, swapped_ref, out_ref):
-    tokens = mine_ref.shape[0]
-    pair = mine_ref[...] + swapped_ref[...]
+def scale_pair(core_ref, both_ref, out_ref):
+    tokens = both_ref.shape[1]
+    pair = both_ref[0] + both_ref[1]
     largest = jnp.max(jnp.abs(pair), axis=0, keepdims=True)
     power = jnp.floor(jnp.log2(jnp.maximum(largest, 1e-30)))
     out_ref[:tokens, :] = pair * jnp.exp2(-power) * 2.0**TOP
@@ -174,9 +151,10 @@
     rows = 2 * columns * own
     shape = jax.ShapeDtypeStruct
 
-    line = spread(jnp.concatenate([inputs, cotangent], axis=0), "col").reshape(columns, 2 * own, depth)
+    block = jnp.concatenate([inputs, cotangent], axis=0)
     core = lax.axis_index("core").astype(jnp.int32).reshape(1)
-    line, core, flipped = lax.optimization_barrier((line, core, 1 - core))
+    block, core = lax.optimization_barrier((block, core))
+    line = spread(block, "col").reshape(columns, 2 * own, depth)
     copies = call(
         split_line,
         shape((planes, rows, depth), BF16),
@@ -186,14 +164,24 @@
     )(line)
     plane = exchange(copies, DP).reshape(planes, rows, depth)
 
-    other = run_forward(flipped, plane, gate_weight, up_weight, down_weight)
-    swapped = lax.ppermute(other, "core", [(0, 1), (1, 0)])
-    mine = run_forward(core, plane, gate_weight, up_weight, down_weight)
+    partial = call(
+        forward,
+        shape((tokens, 3 * width), F32),
+        (6 * tokens * depth * width, plane.size * 2 + 6 * depth * width),
+    )(plane, gate_weight, up_weight, down_weight)
+    both = lax.all_gather(partial, "core", axis=0, tiled=False)
+    half = tokens // 2
     scaled = call(
         scale_pair,
-        shape((tokens // 2 + EXTRA, 3 * width), F32),
+        shape((half + EXTRA, 3 * width), F32),
         (tokens * width * 10, tokens * width * 18),
-    )(mine, swapped).astype(F16)
+        grid_spec=pltpu.PrefetchScalarGridSpec(
+            num_scalar_prefetch=1,
+            grid=(1,),
+            in_specs=[pl.BlockSpec((2, half, 3 * width), lambda i, c: (0, c[0], 0))],
+            out_specs=pl.BlockSpec((half + EXTRA, 3 * width), lambda i, c: (0, 0)),
+        ),
+    )(core, both).astype(F16)
     parts = spread(scaled, "z_hi").reshape((lax.axis_size("z_hi"),) + scaled.shape)
 
     triple = call(activate, shape((tokens // 2, 3 * width), BF16), (tokens * width * 10, parts.size * 4))(parts.astype(F32))

time: 116 us -> 113 us (0.974)
  blocking collectives: 75.3 us -> 95.2 us
  starting transfers between devices: 16.4 us -> 5.3 us
  waiting for transfers between devices: 15.1 us -> 5.12 us
    all_to_all x3 -> x4, blocking collectives: 73.4 us -> 90.9 us  [exchange(): return lax.all_to_all(pieces, axes, split_axis=0, concat_axis=0, tiled=True)]
    all_to_all x2 -> x1, starting transfers between devices: 14.5 us -> 5.3 us  [exchange(): return lax.all_to_all(pieces, axes, split_axis=0, concat_axis=0, tiled=True)]
    all_to_all x2 -> x1, waiting for transfers between devices: 14.2 us -> 5.12 us  [exchange(): return lax.all_to_all(pieces, axes, split_axis=0, concat_axis=0, tiled=True)]
    all_gather x0 -> x1, blocking collectives: none -> 2.37 us  [body(): both = lax.all_gather(partial, 'core', axis=0, tiled=False)]
    ppermute x1 -> x0, starting transfers between devices: 1.92 us -> none  [body(): swapped = lax.ppermute(other, 'core', [(0, 1), (1, 0)])]
  transfers between devices with their start and end apart: 3 -> 1, of which waited for: 3 -> 1; matrix products, arithmetic and copies ran while one was open for 0% -> 0% of each run, Pallas kernels for 3% -> 2%
where the time goes in v6:
time: 113 us
  blocking collectives  95.2 us (84%)
  Pallas kernels  5.58 us (5%)
  starting transfers between devices  5.3 us (5%)
  waiting for transfers between devices  5.12 us (5%)
    all_to_all x4, blocking collectives, exchange(): return lax.all_to_all(pieces, axes, split_axis=0, concat_axis=0, tiled=True)  90.9 us
    all_to_all x1, starting transfers between devices, exchange(): return lax.all_to_all(pieces, axes, split_axis=0, concat_axis=0, tiled=True)  5.3 us
    all_to_all x1, waiting for transfers between devices, exchange(): return lax.all_to_all(pieces, axes, split_axis=0, concat_axis=0, tiled=True)  5.12 us
    pallas_call x1, Pallas kernels, body(): call(weight_grads, [shape(w.shape, BF16) for w in (gate_weight, up_weight...  2.53 us
    all_gather x1, blocking collectives, body(): both = lax.all_gather(partial, 'core', axis=0, tiled=False)  2.37 us
  transfers between devices with their start and end apart: 1, of which 1 were waited for; matrix products, arithmetic and copies ran while one was open for 0% of the time, Pallas kernels for 2%

profile of v6, /device:TPU:8, one launch (start us, length us, event | category | flops | bytes accessed | tf_op | source)
XLA Modules:
  0.0 112.9 jit_solution(14899714358429278262)
XLA Ops:
  0.6 0.8 pad_maximum_fusion
  1.4 17.8 %all_to_all.25.line_ref = bf16[8,8,2048]{2,1,0:T(8,128)(2,1)S(1)} all-to-all(bf16[8,8,2048]{2,1,0:T(8,128)(2,1)S(1)} %broadcast_in_dim.4), channel_id=1, replica_groups=mesh['z_lo'=2,'x'=4,'z_hi'=4,'core'=2,'col'=8] {'col'}, dimensions={0} | all-to-all | bytes 524288 | tf_op jit(solution)/shard_map/all_to_all | solution.py:23
  19.2 0.3 shard_map.84
  19.5 0.0 copy-start
  19.5 0.0 copy-start.1
  19.5 0.0 copy-start.2
  19.5 30.6 %all_to_all.26.plane_ref = bf16[8,64,2048]{2,1,0:T(8,128)(2,1)S(1)} all-to-all(bf16[8,64,2048]{2,1,0:T(8,128)(2,1)S(1)} %shard_map.84), channel_id=1, replica_groups=mesh['z_lo'=2,'x'=4,'z_hi'=4,'core'=2,'col'=8] {'z_lo','x'}, dimensions={0} | all-to-all | bytes 4194304 | tf_op jit(solution)/shard_map/all_to_all | solution.py:23
  50.1 0.0 copy-done
  50.1 0.0 copy-done.1
  50.1 0.0 copy-done.2
  50.1 0.7 shard_map.85
  50.8 2.4 %all-gather = f32[512,384]{1,0:T(8,128)S(1)} all-gather(f32[256,384]{1,0:T(8,128)S(1)} %shard_map.85), channel_id=2, replica_groups=mesh['z_lo'=2,'x'=4,'z_hi'=4,'core'=2,'col'=8] {'core'}, dimensions={0}, use_global_device_ids=true | all-gather | bytes 1179648 | tf_op jit(solution)/shard_map/all_gather | solution.py:172
  53.2 0.1 shard_map.86
  53.3 23.7 %all_to_all.27 = f16[4,136,384]{2,1,0:T(8,128)(2,1)S(1)} all-to-all(f16[4,136,384]{2,1,0:T(8,128)(2,1)S(1)} %broadcast_in_dim.5), channel_id=1, replica_groups=mesh['z_lo'=2,'x'=4,'z_hi'=4,'core'=2,'col'=8] {'z_hi'}, dimensions={0} | all-to-all | bytes 835584 | tf_op jit(solution)/shard_map/all_to_all | solution.py:23
  77.1 0.1 convert_element_type.7.parts_ref
  77.1 0.1 shard_map.87
  77.2 1.9 %all_gather.11.triple_ref = bf16[256,384]{1,0:T(8,128)(2,1)S(1)} all-gather(bf16[128,384]{1,0:T(8,128)(2,1)S(1)} %shard_map.87), channel_id=1, replica_groups=mesh['z_lo'=2,'x'=4,'z_hi'=4,'core'=2,'col'=8] {'core'}, dimensions={0}, use_global_device_ids=true | all-gather | bytes 294912 | tf_op jit(solution)/shard_map/all_gather | solution.py:188
  79.2 0.5 shard_map.88
  79.6 18.9 %all_to_all.28.pieces_ref = bf16[8,32,2048]{2,1,0:T(8,128)(2,1)S(1)} all-to-all(bf16[8,32,2048]{2,1,0:T(8,128)(2,1)S(1)} %shard_map.88), channel_id=1, replica_groups=mesh['z_lo'=2,'x'=4,'z_hi'=4,'core'=2,'col'=8] {'z_lo','x'}, dimensions={0} | all-to-all | bytes 2097152 | tf_op jit(solution)/shard_map/all_to_all | solution.py:23
  98.5 0.8 shard_map.89
  99.3 5.3 %all-to-all-start.4 = ((bf16[8,8,1024]{2,1,0:T(8,128)(2,1)}), bf16[8,8,1024]{2,1,0:T(8,128)(2,1)S(1)}, u32[]{:S(2)}, u32[]{:S(2)}) async-start(bf16[8,8,1024]{2,1,0:T(8,128)(2,1)} %bitcast.2), calls=%async_computation.4 | async-start | bytes 262144 | tf_op jit(solution)/shard_map/all_to_all | solution.py:23
  104.6 2.5 %shard_map.91 = (bf16[2048,128]{1,0:T(8,128)(2,1)}, bf16[2048,128]{1,0:T(8,128)(2,1)}, bf16[128,2048]{1,0:T(8,128)(2,1)}) custom-call(bf16[256,384]{1,0:T(8,128)(2,1)S(1)} %all_gather.11.triple_ref, bf16[8,64,2048]{2,1,0:T(8,128)(2,1)S(1)} %all_to_all.26.plane_ref), custom_call_target="tpu_custom_call" | custom-call | flops 402653184 | bytes 3670016 | tf_op jit(solution)/shard_map/pallas_call | solution.py:203
  107.1 5.1 %all-to-all-done.4.pieces_ref = bf16[8,8,1024]{2,1,0:T(8,128)(2,1)S(1)} async-done(((bf16[8,8,1024]{2,1,0:T(8,128)(2,1)}), bf16[8,8,1024]{2,1,0:T(8,128)(2,1)S(1)}, u32[]{:S(2)}, u32[]{:S(2)}) %all-to-all-start.4) | async-done | bytes 131104 | tf_op jit(solution)/shard_map/all_to_all | solution.py:23
  112.3 0.6 shard_map.90
  (3 shorter events, 0.1 us)
Async XLA Ops:
  19.5 30.6 %copy-start = (bf16[2048,128]{1,0:T(8,128)(2,1)S(1)}, bf16[2048,128]{1,0:T(8,128)(2,1)}, u32[]{:S(2)}) copy-start(bf16[2048,128]{1,0:T(8,128)(2,1)} %gate_ref.3) | copy-start | bytes 1572868
  19.5 30.6 %copy-start.1 = (bf16[2048,128]{1,0:T(8,128)(2,1)S(1)}, bf16[2048,128]{1,0:T(8,128)(2,1)}, u32[]{:S(2)}) copy-start(bf16[2048,128]{1,0:T(8,128)(2,1)} %up_ref.3) | copy-start | bytes 1572868
  19.5 30.6 %copy-start.2 = (bf16[128,2048]{1,0:T(8,128)(2,1)S(1)}, bf16[128,2048]{1,0:T(8,128)(2,1)}, u32[]{:S(2)}) copy-start(bf16[128,2048]{1,0:T(8,128)(2,1)} %down_ref.1) | copy-start | bytes 1572868
  99.3 12.9 %all-to-all-start.4 = ((bf16[8,8,1024]{2,1,0:T(8,128)(2,1)}), bf16[8,8,1024]{2,1,0:T(8,128)(2,1)S(1)}, u32[]{:S(2)}, u32[]{:S(2)}) async-start(bf16[8,8,1024]{2,1,0:T(8,128)(2,1)} %bitcast.2), calls=%async_computation.4 | async-start | bytes 262144 | tf_op jit(solution)/shard_map/all_to_all | solution.py:23

commit v7 on v6

--- a/solution.py
+++ b/solution.py
@@ -6,7 +6,8 @@
 from jax.sharding import Mesh
 from jax.sharding import PartitionSpec as P
 
-DP = ("z_lo", "x")
+SLAB = ("z_lo", "col")
+PLANES = ("x", "z_lo")
 GROUP = ("z_lo", "x", "col")
 ROW = ("z_hi", "core")
 MIB = 1024 * 1024
@@ -44,11 +45,11 @@
 
 
 def split_line(line_ref, out_ref, kept, sems):
-    columns, _, depth = line_ref.shape
+    count, _, depth = line_ref.shape
     blocks = line_ref[...].astype(F32)
     top = upper((8, depth))
     inputs, cotangents = [], []
-    for j in range(columns // 2):
+    for j in range(count // 2):
         a, b = blocks[2 * j], blocks[2 * j + 1]
         inputs.append(jnp.where(top, a, pltpu.roll(b, 4, 0)))
         cotangents.append(jnp.where(top, pltpu.roll(a, 4, 0), b))
@@ -145,24 +146,25 @@
     own, depth = inputs.shape
     width = gate_weight.shape[1]
     columns = lax.axis_size("col")
-    planes = lax.axis_size(DP)
+    planes = lax.axis_size(PLANES)
+    slabs = lax.axis_size("x")
     groups = columns * planes
     tokens = own * groups
-    rows = 2 * columns * own
+    rows = 2 * tokens // slabs
     shape = jax.ShapeDtypeStruct
 
     block = jnp.concatenate([inputs, cotangent], axis=0)
     core = lax.axis_index("core").astype(jnp.int32).reshape(1)
     block, core = lax.optimization_barrier((block, core))
-    line = spread(block, "col").reshape(columns, 2 * own, depth)
+    line = spread(block, SLAB).reshape(groups // slabs, 2 * own, depth)
     copies = call(
         split_line,
-        shape((planes, rows, depth), BF16),
-        (0, planes * rows * depth * 2),
+        shape((slabs, rows, depth), BF16),
+        (0, slabs * rows * depth * 2),
         out_specs=pl.BlockSpec(memory_space=pl.ANY),
-        scratch_shapes=[pltpu.VMEM((rows, depth), BF16), pltpu.SemaphoreType.DMA((planes,))],
+        scratch_shapes=[pltpu.VMEM((rows, depth), BF16), pltpu.SemaphoreType.DMA((slabs,))],
     )(line)
-    plane = exchange(copies, DP).reshape(planes, rows, depth)
+    plane = exchange(copies, "x").reshape(slabs, rows, depth)
 
     partial = call(
         forward,
@@ -196,7 +198,7 @@
         add_planes,
         shape((columns // 2, 2, 2 * own, depth // 2), BF16),
         (tokens * depth, 2 * tokens * depth),
-    )(exchange(partial_in, DP))
+    )(exchange(partial_in, PLANES))
     line_in, later = lax.optimization_barrier((line_in, triple))
     pieces = exchange(line_in.reshape(columns, 2 * own, depth // 2), "col")
     step = depth // 4
@@ -207,7 +209,7 @@
         grid=(4,),
         in_specs=[
             pl.BlockSpec(triple.shape, lambda n: (0, 0)),
-            pl.BlockSpec((planes, rows, step), lambda n: (0, 0, n)),
+            pl.BlockSpec((slabs, rows, step), lambda n: (0, 0, n)),
         ],
         out_specs=[
             pl.BlockSpec((step, width), lambda n: (n, 0)),

time: 113 us -> 119 us (1.053)
  blocking collectives: 95.2 us -> 101 us
    all_to_all x4, blocking collectives: 90.9 us -> 97.1 us  [exchange(): return lax.all_to_all(pieces, axes, split_axis=0, concat_axis=0, tiled=True)]
where the time goes in v7:
time: 119 us
  blocking collectives  101 us (85%)
  Pallas kernels  5.62 us (5%)
  waiting for transfers between devices  5.09 us (4%)
  starting transfers between devices  4.76 us (4%)
    all_to_all x4, blocking collectives, exchange(): return lax.all_to_all(pieces, axes, split_axis=0, concat_axis=0, tiled=True)  97.1 us
    all_to_all x1, waiting for transfers between devices, exchange(): return lax.all_to_all(pieces, axes, split_axis=0, concat_axis=0, tiled=True)  5.09 us
    all_to_all x1, starting transfers between devices, exchange(): return lax.all_to_all(pieces, axes, split_axis=0, concat_axis=0, tiled=True)  4.76 us
    pallas_call x1, Pallas kernels, body(): call(weight_grads, [shape(w.shape, BF16) for w in (gate_weight, up_weight...  2.53 us
  transfers between devices with their start and end apart: 1, of which 1 were waited for; matrix products, arithmetic and copies ran while one was open for 0% of the time, Pallas kernels for 2%

profile of v7, /device:TPU:8, one launch (start us, length us, event | category | flops | bytes accessed | tf_op | source)
XLA Modules:
  0.0 118.5 jit_solution(10619072406380164719)
XLA Ops:
  0.6 0.8 pad_maximum_fusion
  1.4 24.1 %all_to_all.25.line_ref = bf16[16,8,2048]{2,1,0:T(8,128)(2,1)S(1)} all-to-all(bf16[16,8,2048]{2,1,0:T(8,128)(2,1)S(1)} %broadcast_in_dim.4), channel_id=1, replica_groups=mesh['z_lo'=2,'x'=4,'z_hi'=4,'core'=2,'col'=8] {'z_lo','col'}, dimensions={0} | all-to-all | bytes 1048576 | tf_op jit(solution)/shard_map/all_to_all | solution.py:24
  25.6 0.4 shard_map.84
  26.0 0.0 copy-start
  26.0 0.0 copy-start.1
  26.0 0.0 copy-start.2
  26.0 29.6 %all_to_all.26.plane_ref = bf16[4,128,2048]{2,1,0:T(8,128)(2,1)S(1)} all-to-all(bf16[4,128,2048]{2,1,0:T(8,128)(2,1)S(1)} %shard_map.84), channel_id=1, replica_groups=mesh['z_lo'=2,'x'=4,'z_hi'=4,'core'=2,'col'=8] {'x'}, dimensions={0} | all-to-all | bytes 4194304 | tf_op jit(solution)/shard_map/all_to_all | solution.py:24
  55.6 0.0 copy-done
  55.6 0.0 copy-done.1
  55.6 0.0 copy-done.2
  55.6 0.7 shard_map.85
  56.3 2.4 %all-gather = f32[512,384]{1,0:T(8,128)S(1)} all-gather(f32[256,384]{1,0:T(8,128)S(1)} %shard_map.85), channel_id=2, replica_groups=mesh['z_lo'=2,'x'=4,'z_hi'=4,'core'=2,'col'=8] {'core'}, dimensions={0}, use_global_device_ids=true | all-gather | bytes 1179648 | tf_op jit(solution)/shard_map/all_gather | solution.py:174
  58.7 0.1 shard_map.86
  58.8 24.6 %all_to_all.27 = f16[4,136,384]{2,1,0:T(8,128)(2,1)S(1)} all-to-all(f16[4,136,384]{2,1,0:T(8,128)(2,1)S(1)} %broadcast_in_dim.5), channel_id=1, replica_groups=mesh['z_lo'=2,'x'=4,'z_hi'=4,'core'=2,'col'=8] {'z_hi'}, dimensions={0} | all-to-all | bytes 835584 | tf_op jit(solution)/shard_map/all_to_all | solution.py:24
  83.4 0.1 convert_element_type.7.parts_ref
  83.5 0.1 shard_map.87
  83.6 1.9 %all_gather.11.triple_ref = bf16[256,384]{1,0:T(8,128)(2,1)S(1)} all-gather(bf16[128,384]{1,0:T(8,128)(2,1)S(1)} %shard_map.87), channel_id=1, replica_groups=mesh['z_lo'=2,'x'=4,'z_hi'=4,'core'=2,'col'=8] {'core'}, dimensions={0}, use_global_device_ids=true | all-gather | bytes 294912 | tf_op jit(solution)/shard_map/all_gather | solution.py:190
  85.5 0.5 shard_map.88
  86.0 18.7 %all_to_all.28.pieces_ref = bf16[8,32,2048]{2,1,0:T(8,128)(2,1)S(1)} all-to-all(bf16[8,32,2048]{2,1,0:T(8,128)(2,1)S(1)} %shard_map.88), channel_id=1, replica_groups=mesh['z_lo'=2,'x'=4,'z_hi'=4,'core'=2,'col'=8] {'x','z_lo'}, dimensions={0} | all-to-all | bytes 2097152 | tf_op jit(solution)/shard_map/all_to_all | solution.py:24
  104.7 0.8 shard_map.89
  105.5 4.8 %all-to-all-start.4 = ((bf16[8,8,1024]{2,1,0:T(8,128)(2,1)}), bf16[8,8,1024]{2,1,0:T(8,128)(2,1)S(1)}, u32[]{:S(2)}, u32[]{:S(2)}) async-start(bf16[8,8,1024]{2,1,0:T(8,128)(2,1)} %bitcast.2), calls=%async_computation.4 | async-start | bytes 262144 | tf_op jit(solution)/shard_map/all_to_all | solution.py:24
  110.3 2.5 %shard_map.91 = (bf16[2048,128]{1,0:T(8,128)(2,1)}, bf16[2048,128]{1,0:T(8,128)(2,1)}, bf16[128,2048]{1,0:T(8,128)(2,1)}) custom-call(bf16[256,384]{1,0:T(8,128)(2,1)S(1)} %all_gather.11.triple_ref, bf16[4,128,2048]{2,1,0:T(8,128)(2,1)S(1)} %all_to_all.26.plane_ref), custom_call_target="tpu_custom_call" | custom-call | flops 402653184 | bytes 3670016 | tf_op jit(solution)/shard_map/pallas_call | solution.py:205
  112.8 5.1 %all-to-all-done.4.pieces_ref = bf16[8,8,1024]{2,1,0:T(8,128)(2,1)S(1)} async-done(((bf16[8,8,1024]{2,1,0:T(8,128)(2,1)}), bf16[8,8,1024]{2,1,0:T(8,128)(2,1)S(1)}, u32[]{:S(2)}, u32[]{:S(2)}) %all-to-all-start.4) | async-done | bytes 131104 | tf_op jit(solution)/shard_map/all_to_all | solution.py:24
  117.9 0.6 shard_map.90
  (3 shorter events, 0.1 us)
Async XLA Ops:
  26.0 29.6 %copy-start = (bf16[2048,128]{1,0:T(8,128)(2,1)S(1)}, bf16[2048,128]{1,0:T(8,128)(2,1)}, u32[]{:S(2)}) copy-start(bf16[2048,128]{1,0:T(8,128)(2,1)} %gate_ref.3) | copy-start | bytes 1572868
  26.0 29.6 %copy-start.1 = (bf16[2048,128]{1,0:T(8,128)(2,1)S(1)}, bf16[2048,128]{1,0:T(8,128)(2,1)}, u32[]{:S(2)}) copy-start(bf16[2048,128]{1,0:T(8,128)(2,1)} %up_ref.3) | copy-start | bytes 1572868
  26.0 29.6 %copy-start.2 = (bf16[128,2048]{1,0:T(8,128)(2,1)S(1)}, bf16[128,2048]{1,0:T(8,128)(2,1)}, u32[]{:S(2)}) copy-start(bf16[128,2048]{1,0:T(8,128)(2,1)} %down_ref.1) | copy-start | bytes 1572868
  105.5 12.4 %all-to-all-start.4 = ((bf16[8,8,1024]{2,1,0:T(8,128)(2,1)}), bf16[8,8,1024]{2,1,0:T(8,128)(2,1)S(1)}, u32[]{:S(2)}, u32[]{:S(2)}) async-start(bf16[8,8,1024]{2,1,0:T(8,128)(2,1)} %bitcast.2), calls=%async_computation.4 | async-start | bytes 262144 | tf_op jit(solution)/shard_map/all_to_all | solution.py:24

commit v8 on v6

--- a/solution.py
+++ b/solution.py
@@ -9,6 +9,8 @@
 DP = ("z_lo", "x")
 GROUP = ("z_lo", "x", "col")
 ROW = ("z_hi", "core")
+FIRST_PAIRS = ((0, 1), (2, 3))
+SECOND_PAIRS = ((0, 3), (1, 2))
 MIB = 1024 * 1024
 EXTRA = 8
 TOP = 14
@@ -71,22 +73,34 @@
     out_ref[:, 2 * width :] = lax.dot_general(cotangents, down_ref[...], LAST, preferred_element_type=F32)
 
 
-def scale_pair(core_ref, both_ref, out_ref):
-    tokens = both_ref.shape[1]
-    pair = both_ref[0] + both_ref[1]
+def store_scaled(pair, out_ref):
+    tokens = pair.shape[0]
     largest = jnp.max(jnp.abs(pair), axis=0, keepdims=True)
     power = jnp.floor(jnp.log2(jnp.maximum(largest, 1e-30)))
     out_ref[:tokens, :] = pair * jnp.exp2(-power) * 2.0**TOP
     out_ref[tokens:, :] = jnp.broadcast_to(power, (EXTRA, pair.shape[1]))
 
 
-def activate(parts_ref, out_ref):
-    tokens = out_ref.shape[0]
-    width = out_ref.shape[1] // 3
+def sum_scaled(parts_ref):
+    tokens = parts_ref.shape[1] - EXTRA
     summed = 0.0
     for z in range(parts_ref.shape[0]):
         power = parts_ref[z, tokens:, :][:1]
         summed = summed + parts_ref[z, :tokens, :] * (jnp.exp2(power) * 2.0**-TOP)
+    return summed
+
+
+def scale_pair(core_ref, both_ref, out_ref):
+    store_scaled(both_ref[0] + both_ref[1], out_ref)
+
+
+def rescale(parts_ref, out_ref):
+    store_scaled(sum_scaled(parts_ref), out_ref)
+
+
+def activate(parts_ref, out_ref):
+    width = out_ref.shape[1] // 3
+    summed = sum_scaled(parts_ref)
     gate = summed[:, :width]
     up = summed[:, width : 2 * width]
     hidden_grad = summed[:, 2 * width :]
@@ -182,7 +196,9 @@
             out_specs=pl.BlockSpec((half + EXTRA, 3 * width), lambda i, c: (0, 0)),
         ),
     )(core, both).astype(F16)
-    parts = spread(scaled, "z_hi").reshape((lax.axis_size("z_hi"),) + scaled.shape)
+    parts = lax.all_gather(scaled, "z_hi", axis=0, tiled=False, axis_index_groups=FIRST_PAIRS)
+    scaled = call(rescale, shape(scaled.shape, F32), (tokens * width * 10, parts.size * 4))(parts.astype(F32)).astype(F16)
+    parts = lax.all_gather(scaled, "z_hi", axis=0, tiled=False, axis_index_groups=SECOND_PAIRS)
 
     triple = call(activate, shape((tokens // 2, 3 * width), BF16), (tokens * width * 10, parts.size * 4))(parts.astype(F32))
     triple = lax.all_gather(triple, "core", axis=0, tiled=True)

time: 113 us -> 110 us (0.973)
  blocking collectives: 95.2 us -> 91.7 us
    all_to_all x4 -> x3, blocking collectives: 90.9 us -> 68.6 us  [exchange(): return lax.all_to_all(pieces, axes, split_axis=0, concat_axis=0, tiled=True)]
    all_gather x0 -> x2, blocking collectives: none -> 18.8 us  [the longest x1 10.3 us: body(): lax.all_gather(scaled, 'z_hi', axis=0, tiled=False, axis_index_groups=FIR...]
where the time goes in v8:
time: 110 us
  blocking collectives  91.7 us (83%)
  Pallas kernels  5.62 us (5%)
  starting transfers between devices  5.48 us (5%)
  waiting for transfers between devices  5.12 us (5%)
    all_to_all x3, blocking collectives, exchange(): return lax.all_to_all(pieces, axes, split_axis=0, concat_axis=0, tiled=True)  68.6 us
    all_gather x1, blocking collectives, body(): lax.all_gather(scaled, 'z_hi', axis=0, tiled=False, axis_index_groups=FIR...  10.3 us
    all_gather x1, blocking collectives, body(): lax.all_gather(scaled, 'z_hi', axis=0, tiled=False, axis_index_groups=SEC...  8.5 us
    all_to_all x1, starting transfers between devices, exchange(): return lax.all_to_all(pieces, axes, split_axis=0, concat_axis=0, tiled=True)  5.48 us
    all_to_all x1, waiting for transfers between devices, exchange(): return lax.all_to_all(pieces, axes, split_axis=0, concat_axis=0, tiled=True)  5.12 us
    pallas_call x1, Pallas kernels, body(): call(weight_grads, [shape(w.shape, BF16) for w in (gate_weight, up_weight...  2.53 us
    all_gather x1, blocking collectives, body(): both = lax.all_gather(partial, 'core', axis=0, tiled=False)  2.37 us
  transfers between devices with their start and end apart: 1, of which 1 were waited for; matrix products, arithmetic and copies ran while one was open for 0% of the time, Pallas kernels for 2%

profile of v8, /device:TPU:8, one launch (start us, length us, event | category | flops | bytes accessed | tf_op | source)
XLA Modules:
  0.0 109.6 jit_solution(9166671167096693209)
XLA Ops:
  0.6 0.8 pad_maximum_fusion
  1.4 17.8 %all_to_all.20.line_ref = bf16[8,8,2048]{2,1,0:T(8,128)(2,1)S(1)} all-to-all(bf16[8,8,2048]{2,1,0:T(8,128)(2,1)S(1)} %broadcast_in_dim.2), channel_id=1, replica_groups=mesh['z_lo'=2,'x'=4,'z_hi'=4,'core'=2,'col'=8] {'col'}, dimensions={0} | all-to-all | bytes 524288 | tf_op jit(solution)/shard_map/all_to_all | solution.py:25
  19.2 0.3 shard_map.84
  19.5 0.0 copy-start
  19.5 0.0 copy-start.1
  19.5 0.0 copy-start.2
  19.5 30.6 %all_to_all.21.plane_ref = bf16[8,64,2048]{2,1,0:T(8,128)(2,1)S(1)} all-to-all(bf16[8,64,2048]{2,1,0:T(8,128)(2,1)S(1)} %shard_map.84), channel_id=1, replica_groups=mesh['z_lo'=2,'x'=4,'z_hi'=4,'core'=2,'col'=8] {'z_lo','x'}, dimensions={0} | all-to-all | bytes 4194304 | tf_op jit(solution)/shard_map/all_to_all | solution.py:25
  50.1 0.0 copy-done
  50.1 0.0 copy-done.1
  50.1 0.0 copy-done.2
  50.1 0.7 shard_map.85
  50.8 2.4 %all-gather = f32[512,384]{1,0:T(8,128)S(1)} all-gather(f32[256,384]{1,0:T(8,128)S(1)} %shard_map.85), channel_id=2, replica_groups=mesh['z_lo'=2,'x'=4,'z_hi'=4,'core'=2,'col'=8] {'core'}, dimensions={0}, use_global_device_ids=true | all-gather | bytes 1179648 | tf_op jit(solution)/shard_map/all_gather | solution.py:186
  53.2 0.1 shard_map.86
  53.3 10.3 %all-gather.1 = f16[272,384]{1,0:T(8,128)(2,1)S(1)} all-gather(f16[136,384]{1,0:T(8,128)(2,1)S(1)} %convert_element_type.12), channel_id=3, replica_groups={{0,16},{32,48},{1,17},{33,49},{2,18},{34,50},{3,19},{35,51},{4,20},{36,..., dimensions={0}, use_global_device_ids=true | all-gather | bytes 313344 | tf_op jit(solution)/shard_map/all_gather | solution.py:199
  63.6 0.1 shard_map.87
  63.7 8.5 %all-gather.2 = f16[272,384]{1,0:T(8,128)(2,1)S(1)} all-gather(f16[136,384]{1,0:T(8,128)(2,1)S(1)} %convert_element_type.14), channel_id=4, replica_groups={{0,48},{16,32},{1,49},{17,33},{2,50},{18,34},{3,51},{19,35},{4,52},{20,..., dimensions={0}, use_global_device_ids=true | all-gather | bytes 313344 | tf_op jit(solution)/shard_map/all_gather | solution.py:201
  72.2 0.1 shard_map.88
  72.3 1.9 %all_gather.27.triple_ref = bf16[256,384]{1,0:T(8,128)(2,1)S(1)} all-gather(bf16[128,384]{1,0:T(8,128)(2,1)S(1)} %shard_map.88), channel_id=1, replica_groups=mesh['z_lo'=2,'x'=4,'z_hi'=4,'core'=2,'col'=8] {'core'}, dimensions={0}, use_global_device_ids=true | all-gather | bytes 294912 | tf_op jit(solution)/shard_map/all_gather | solution.py:204
  74.3 0.5 shard_map.89
  74.7 20.3 %all_to_all.22.pieces_ref = bf16[8,32,2048]{2,1,0:T(8,128)(2,1)S(1)} all-to-all(bf16[8,32,2048]{2,1,0:T(8,128)(2,1)S(1)} %shard_map.89), channel_id=1, replica_groups=mesh['z_lo'=2,'x'=4,'z_hi'=4,'core'=2,'col'=8] {'z_lo','x'}, dimensions={0} | all-to-all | bytes 2097152 | tf_op jit(solution)/shard_map/all_to_all | solution.py:25
  95.0 0.8 shard_map.90
  95.8 5.5 %all-to-all-start.3 = ((bf16[8,8,1024]{2,1,0:T(8,128)(2,1)}), bf16[8,8,1024]{2,1,0:T(8,128)(2,1)S(1)}, u32[]{:S(2)}, u32[]{:S(2)}) async-start(bf16[8,8,1024]{2,1,0:T(8,128)(2,1)} %bitcast.4), calls=%async_computation.3 | async-start | bytes 262144 | tf_op jit(solution)/shard_map/all_to_all | solution.py:25
  101.3 2.5 %shard_map.92 = (bf16[2048,128]{1,0:T(8,128)(2,1)}, bf16[2048,128]{1,0:T(8,128)(2,1)}, bf16[128,2048]{1,0:T(8,128)(2,1)}) custom-call(bf16[256,384]{1,0:T(8,128)(2,1)S(1)} %all_gather.27.triple_ref, bf16[8,64,2048]{2,1,0:T(8,128)(2,1)S(1)} %all_to_all.21.plane_ref), custom_call_target="tpu_custom_call" | custom-call | flops 402653184 | bytes 3670016 | tf_op jit(solution)/shard_map/pallas_call | solution.py:219
  103.8 5.1 %all-to-all-done.3.pieces_ref = bf16[8,8,1024]{2,1,0:T(8,128)(2,1)S(1)} async-done(((bf16[8,8,1024]{2,1,0:T(8,128)(2,1)}), bf16[8,8,1024]{2,1,0:T(8,128)(2,1)S(1)}, u32[]{:S(2)}, u32[]{:S(2)}) %all-to-all-start.3) | async-done | bytes 131104 | tf_op jit(solution)/shard_map/all_to_all | solution.py:25
  108.9 0.6 shard_map.91
  (5 shorter events, 0.1 us)
Async XLA Ops:
  19.5 30.6 %copy-start = (bf16[2048,128]{1,0:T(8,128)(2,1)S(1)}, bf16[2048,128]{1,0:T(8,128)(2,1)}, u32[]{:S(2)}) copy-start(bf16[2048,128]{1,0:T(8,128)(2,1)} %gate_ref.3) | copy-start | bytes 1572868
  19.5 30.6 %copy-start.1 = (bf16[2048,128]{1,0:T(8,128)(2,1)S(1)}, bf16[2048,128]{1,0:T(8,128)(2,1)}, u32[]{:S(2)}) copy-start(bf16[2048,128]{1,0:T(8,128)(2,1)} %up_ref.3) | copy-start | bytes 1572868
  19.5 30.6 %copy-start.2 = (bf16[128,2048]{1,0:T(8,128)(2,1)S(1)}, bf16[128,2048]{1,0:T(8,128)(2,1)}, u32[]{:S(2)}) copy-start(bf16[128,2048]{1,0:T(8,128)(2,1)} %down_ref.1) | copy-start | bytes 1572868
  95.8 13.1 %all-to-all-start.3 = ((bf16[8,8,1024]{2,1,0:T(8,128)(2,1)}), bf16[8,8,1024]{2,1,0:T(8,128)(2,1)S(1)}, u32[]{:S(2)}, u32[]{:S(2)}) async-start(bf16[8,8,1024]{2,1,0:T(8,128)(2,1)} %bitcast.4), calls=%async_computation.3 | async-start | bytes 262144 | tf_op jit(solution)/shard_map/all_to_all | solution.py:25

commit v9 on v8

--- a/solution.py
+++ b/solution.py
@@ -7,7 +7,9 @@
 from jax.sharding import PartitionSpec as P
 
 DP = ("z_lo", "x")
-GROUP = ("z_lo", "x", "col")
+NEAR = ("z_lo", "x", "y_lo")
+COLUMN = ("y_lo", "y_hi")
+GROUP = ("z_lo", "x", "y_hi", "y_lo")
 ROW = ("z_hi", "core")
 FIRST_PAIRS = ((0, 1), (2, 3))
 SECOND_PAIRS = ((0, 3), (1, 2))
@@ -45,7 +47,7 @@
     return lax.broadcasted_iota(jnp.int32, shape, len(shape) - 2) < 4
 
 
-def split_line(line_ref, out_ref, kept, sems):
+def split_line(line_ref, out_ref):
     columns, _, depth = line_ref.shape
     blocks = line_ref[...].astype(F32)
     top = upper((8, depth))
@@ -54,12 +56,9 @@
         a, b = blocks[2 * j], blocks[2 * j + 1]
         inputs.append(jnp.where(top, a, pltpu.roll(b, 4, 0)))
         cotangents.append(jnp.where(top, pltpu.roll(a, 4, 0), b))
-    kept[...] = jnp.concatenate(inputs + cotangents, axis=0).astype(BF16)
-    copies = [pltpu.make_async_copy(kept, out_ref.at[p], sems.at[p]) for p in range(out_ref.shape[0])]
-    for copy in copies:
-        copy.start()
-    for copy in copies:
-        copy.wait()
+    rows = jnp.concatenate(inputs + cotangents, axis=0).astype(BF16)
+    for p in range(out_ref.shape[0]):
+        out_ref[p] = rows
 
 
 def forward(plane_ref, gate_ref, up_ref, down_ref, out_ref):
@@ -158,25 +157,24 @@
 def body(inputs, cotangent, gate_weight, up_weight, down_weight):
     own, depth = inputs.shape
     width = gate_weight.shape[1]
-    columns = lax.axis_size("col")
+    columns = lax.axis_size(COLUMN)
     planes = lax.axis_size(DP)
     groups = columns * planes
     tokens = own * groups
-    rows = 2 * columns * own
+    near = lax.axis_size(NEAR)
+    rows = 2 * tokens // near
     shape = jax.ShapeDtypeStruct
 
     block = jnp.concatenate([inputs, cotangent], axis=0)
     core = lax.axis_index("core").astype(jnp.int32).reshape(1)
     block, core = lax.optimization_barrier((block, core))
-    line = spread(block, "col").reshape(columns, 2 * own, depth)
+    line = spread(block, "y_hi").reshape(groups // near, 2 * own, depth)
     copies = call(
         split_line,
-        shape((planes, rows, depth), BF16),
-        (0, planes * rows * depth * 2),
-        out_specs=pl.BlockSpec(memory_space=pl.ANY),
-        scratch_shapes=[pltpu.VMEM((rows, depth), BF16), pltpu.SemaphoreType.DMA((planes,))],
+        shape((near, rows, depth), BF16),
+        (0, near * rows * depth * 2),
     )(line)
-    plane = exchange(copies, DP).reshape(planes, rows, depth)
+    plane = exchange(copies, NEAR).reshape(near, rows, depth)
 
     partial = call(
         forward,
@@ -214,7 +212,7 @@
         (tokens * depth, 2 * tokens * depth),
     )(exchange(partial_in, DP))
     line_in, later = lax.optimization_barrier((line_in, triple))
-    pieces = exchange(line_in.reshape(columns, 2 * own, depth // 2), "col")
+    pieces = exchange(line_in.reshape(columns, 2 * own, depth // 2), COLUMN)
     step = depth // 4
     grad_gate_weight, grad_up_weight, grad_down_weight = call(
         weight_grads,
@@ -223,7 +221,7 @@
         grid=(4,),
         in_specs=[
             pl.BlockSpec(triple.shape, lambda n: (0, 0)),
-            pl.BlockSpec((planes, rows, step), lambda n: (0, 0, n)),
+            pl.BlockSpec((near, rows, step), lambda n: (0, 0, n)),
         ],
         out_specs=[
             pl.BlockSpec((step, width), lambda n: (n, 0)),
@@ -236,7 +234,7 @@
 
 
 def solution(mesh):
-    fine = Mesh(mesh.devices.reshape(2, 4, 4, 2, 8), ("z_lo", "x", "z_hi", "core", "col"))
+    fine = Mesh(mesh.devices.reshape(2, 4, 4, 2, 4, 2), ("z_lo", "x", "z_hi", "core", "y_hi", "y_lo"))
     in_specs = (P(GROUP, ROW), P(GROUP, ROW), P(ROW, GROUP), P(ROW, GROUP), P(GROUP, ROW))
     out_specs = (P(GROUP, ROW), P(ROW, GROUP), P(ROW, GROUP), P(GROUP, ROW))
     return jax.shard_map(body, mesh=fine, in_specs=in_specs, out_specs=out_specs, check_vma=False)

time: 110 us -> 108 us (0.982)
  no operation moved by 1% of the time
where the time goes in v9:
time: 108 us
  blocking collectives  91 us (84%)
  Pallas kernels  5.5 us (5%)
  waiting for transfers between devices  5.09 us (5%)
  starting transfers between devices  4.5 us (4%)
    all_to_all x3, blocking collectives, exchange(): return lax.all_to_all(pieces, axes, split_axis=0, concat_axis=0, tiled=True)  68.5 us
    all_gather x1, blocking collectives, body(): lax.all_gather(scaled, 'z_hi', axis=0, tiled=False, axis_index_groups=FIR...  10.3 us
    all_gather x1, blocking collectives, body(): lax.all_gather(scaled, 'z_hi', axis=0, tiled=False, axis_index_groups=SEC...  7.87 us
    all_to_all x1, waiting for transfers between devices, exchange(): return lax.all_to_all(pieces, axes, split_axis=0, concat_axis=0, tiled=True)  5.09 us
    all_to_all x1, starting transfers between devices, exchange(): return lax.all_to_all(pieces, axes, split_axis=0, concat_axis=0, tiled=True)  4.5 us
    pallas_call x1, Pallas kernels, body(): call(weight_grads, [shape(w.shape, BF16) for w in (gate_weight, up_weight...  2.53 us
    all_gather x1, blocking collectives, body(): both = lax.all_gather(partial, 'core', axis=0, tiled=False)  2.37 us
  transfers between devices with their start and end apart: 1, of which 1 were waited for; matrix products, arithmetic and copies ran while one was open for 0% of the time, Pallas kernels for 2%

profile of v9, /device:TPU:8, one launch (start us, length us, event | category | flops | bytes accessed | tf_op | source)
XLA Modules:
  0.0 107.7 jit_solution(11185221180302690060)
XLA Ops:
  0.6 0.8 pad_maximum_fusion
  1.4 14.5 %all_to_all.20.line_ref = bf16[4,8,2048]{2,1,0:T(8,128)(2,1)S(1)} all-to-all(bf16[4,8,2048]{2,1,0:T(8,128)(2,1)S(1)} %broadcast_in_dim.2), channel_id=1, replica_groups=mesh['z_lo'=2,'x'=4,'z_hi'=4,'core'=2,'y_hi'=4,'y_lo'=2] {'y_hi'}, dimensions={0} | all-to-all | bytes 262144 | tf_op jit(solution)/shard_map/all_to_all | solution.py:27
  15.9 0.2 shard_map.84
  16.1 0.0 copy-start
  16.1 0.0 copy-start.1
  16.1 0.0 copy-start.2
  16.1 32.5 %all_to_all.21.plane_ref = bf16[16,32,2048]{2,1,0:T(8,128)(2,1)S(1)} all-to-all(bf16[16,32,2048]{2,1,0:T(8,128)(2,1)S(1)} %shard_map.84), channel_id=1, replica_groups=mesh['z_lo'=2,'x'=4,'z_hi'=4,'core'=2,'y_hi'=4,'y_lo'=2] {'z_lo','x','y_..., dimensions={0} | all-to-all | bytes 4194304 | tf_op jit(solution)/shard_map/all_to_all | solution.py:27
  48.6 0.0 copy-done
  48.6 0.0 copy-done.1
  48.6 0.0 copy-done.2
  48.6 0.7 shard_map.85
  49.3 2.4 %all-gather = f32[512,384]{1,0:T(8,128)S(1)} all-gather(f32[256,384]{1,0:T(8,128)S(1)} %shard_map.85), channel_id=2, replica_groups=mesh['z_lo'=2,'x'=4,'z_hi'=4,'core'=2,'y_hi'=4,'y_lo'=2] {'core'}, dimensions={0}, use_global_device_ids=true | all-gather | bytes 1179648 | tf_op jit(solution)/shard_map/all_gather | solution.py:184
  51.7 0.1 shard_map.86
  51.8 10.3 %all-gather.1 = f16[272,384]{1,0:T(8,128)(2,1)S(1)} all-gather(f16[136,384]{1,0:T(8,128)(2,1)S(1)} %convert_element_type.12), channel_id=3, replica_groups={{0,16},{32,48},{1,17},{33,49},{2,18},{34,50},{3,19},{35,51},{4,20},{36,..., dimensions={0}, use_global_device_ids=true | all-gather | bytes 313344 | tf_op jit(solution)/shard_map/all_gather | solution.py:197
  62.1 0.1 shard_map.87
  62.2 7.9 %all-gather.2 = f16[272,384]{1,0:T(8,128)(2,1)S(1)} all-gather(f16[136,384]{1,0:T(8,128)(2,1)S(1)} %convert_element_type.14), channel_id=4, replica_groups={{0,48},{16,32},{1,49},{17,33},{2,50},{18,34},{3,51},{19,35},{4,52},{20,..., dimensions={0}, use_global_device_ids=true | all-gather | bytes 313344 | tf_op jit(solution)/shard_map/all_gather | solution.py:199
  70.1 0.1 shard_map.88
  70.2 1.9 %all_gather.27.triple_ref = bf16[256,384]{1,0:T(8,128)(2,1)S(1)} all-gather(bf16[128,384]{1,0:T(8,128)(2,1)S(1)} %shard_map.88), channel_id=1, replica_groups=mesh['z_lo'=2,'x'=4,'z_hi'=4,'core'=2,'y_hi'=4,'y_lo'=2] {'core'}, dimensions={0}, use_global_device_ids=true | all-gather | bytes 294912 | tf_op jit(solution)/shard_map/all_gather | solution.py:202
  72.1 0.5 shard_map.89
  72.6 21.5 %all_to_all.22.pieces_ref = bf16[8,32,2048]{2,1,0:T(8,128)(2,1)S(1)} all-to-all(bf16[8,32,2048]{2,1,0:T(8,128)(2,1)S(1)} %shard_map.89), channel_id=1, replica_groups=mesh['z_lo'=2,'x'=4,'z_hi'=4,'core'=2,'y_hi'=4,'y_lo'=2] {'z_lo','x'}, dimensions={0} | all-to-all | bytes 2097152 | tf_op jit(solution)/shard_map/all_to_all | solution.py:27
  94.1 0.8 shard_map.90
  94.9 4.5 %all-to-all-start.3 = ((bf16[8,8,1024]{2,1,0:T(8,128)(2,1)}), bf16[8,8,1024]{2,1,0:T(8,128)(2,1)S(1)}, u32[]{:S(2)}, u32[]{:S(2)}) async-start(bf16[8,8,1024]{2,1,0:T(8,128)(2,1)} %bitcast.4), calls=%async_computation.3 | async-start | bytes 262144 | tf_op jit(solution)/shard_map/all_to_all | solution.py:27
  99.4 2.5 %shard_map.92 = (bf16[2048,128]{1,0:T(8,128)(2,1)}, bf16[2048,128]{1,0:T(8,128)(2,1)}, bf16[128,2048]{1,0:T(8,128)(2,1)}) custom-call(bf16[256,384]{1,0:T(8,128)(2,1)S(1)} %all_gather.27.triple_ref, bf16[16,32,2048]{2,1,0:T(8,128)(2,1)S(1)} %all_to_all.21.plane_ref), custom_call_target="tpu_custom_call" | custom-call | flops 402653184 | bytes 3670016 | tf_op jit(solution)/shard_map/pallas_call | solution.py:217
  102.0 5.1 %all-to-all-done.3.pieces_ref = bf16[8,8,1024]{2,1,0:T(8,128)(2,1)S(1)} async-done(((bf16[8,8,1024]{2,1,0:T(8,128)(2,1)}), bf16[8,8,1024]{2,1,0:T(8,128)(2,1)S(1)}, u32[]{:S(2)}, u32[]{:S(2)}) %all-to-all-start.3) | async-done | bytes 131104 | tf_op jit(solution)/shard_map/all_to_all | solution.py:27
  107.1 0.6 shard_map.91
  (5 shorter events, 0.1 us)
Async XLA Ops:
  16.1 32.5 %copy-start = (bf16[2048,128]{1,0:T(8,128)(2,1)S(1)}, bf16[2048,128]{1,0:T(8,128)(2,1)}, u32[]{:S(2)}) copy-start(bf16[2048,128]{1,0:T(8,128)(2,1)} %gate_ref.3) | copy-start | bytes 1572868
  16.1 32.5 %copy-start.1 = (bf16[2048,128]{1,0:T(8,128)(2,1)S(1)}, bf16[2048,128]{1,0:T(8,128)(2,1)}, u32[]{:S(2)}) copy-start(bf16[2048,128]{1,0:T(8,128)(2,1)} %up_ref.3) | copy-start | bytes 1572868
  16.1 32.5 %copy-start.2 = (bf16[128,2048]{1,0:T(8,128)(2,1)S(1)}, bf16[128,2048]{1,0:T(8,128)(2,1)}, u32[]{:S(2)}) copy-start(bf16[128,2048]{1,0:T(8,128)(2,1)} %down_ref.1) | copy-start | bytes 1572868
  94.9 12.1 %all-to-all-start.3 = ((bf16[8,8,1024]{2,1,0:T(8,128)(2,1)}), bf16[8,8,1024]{2,1,0:T(8,128)(2,1)S(1)}, u32[]{:S(2)}, u32[]{:S(2)}) async-start(bf16[8,8,1024]{2,1,0:T(8,128)(2,1)} %bitcast.4), calls=%async_computation.3 | async-start | bytes 262144 | tf_op jit(solution)/shard_map/all_to_all | solution.py:27

commit v10 on v9

--- a/solution.py
+++ b/solution.py
@@ -6,8 +6,8 @@
 from jax.sharding import Mesh
 from jax.sharding import PartitionSpec as P
 
-DP = ("z_lo", "x")
-NEAR = ("z_lo", "x", "y_lo")
+DP = ("x", "z_lo")
+NEAR = ("x", "z_lo", "y_lo")
 COLUMN = ("y_lo", "y_hi")
 GROUP = ("z_lo", "x", "y_hi", "y_lo")
 ROW = ("z_hi", "core")
@@ -99,7 +99,7 @@
 
 def activate(parts_ref, out_ref):
     width = out_ref.shape[1] // 3
-    summed = sum_scaled(parts_ref)
+    summed = jnp.concatenate([sum_scaled(parts_ref.at[:, c]) for c in range(2)], axis=0)
     gate = summed[:, :width]
     up = summed[:, width : 2 * width]
     hidden_grad = summed[:, 2 * width :]
@@ -196,10 +196,11 @@
     )(core, both).astype(F16)
     parts = lax.all_gather(scaled, "z_hi", axis=0, tiled=False, axis_index_groups=FIRST_PAIRS)
     scaled = call(rescale, shape(scaled.shape, F32), (tokens * width * 10, parts.size * 4))(parts.astype(F32)).astype(F16)
-    parts = lax.all_gather(scaled, "z_hi", axis=0, tiled=False, axis_index_groups=SECOND_PAIRS)
-
-    triple = call(activate, shape((tokens // 2, 3 * width), BF16), (tokens * width * 10, parts.size * 4))(parts.astype(F32))
-    triple = lax.all_gather(triple, "core", axis=0, tiled=True)
+    quads = tuple(tuple(2 * z + c for z in pair for c in range(2)) for pair in SECOND_PAIRS)
+    parts = lax.all_gather(scaled, ROW, axis=0, tiled=False, axis_index_groups=quads)
+    parts = parts.reshape((2, 2) + scaled.shape)
+
+    triple = call(activate, shape((tokens, 3 * width), BF16), (tokens * width * 20, parts.size * 4))(parts.astype(F32))
 
     partial_in = call(
         input_grads,

time: 108 us -> 108 us (level)
    all_gather x2 -> x1, blocking collectives: 9.82 us -> 9.62 us  [body(): lax.all_gather(scaled, ROW, axis=0, tiled=False, axis_index_groups=quads)]
where the time goes in v10:
time: 108 us; the launch traced here: 107 us
  blocking collectives  90.5 us (84%)
  Pallas kernels  5.57 us (5%)
  waiting for transfers between devices  5.09 us (5%)
  starting transfers between devices  4.36 us (4%)
    all_to_all x3, blocking collectives, exchange(): return lax.all_to_all(pieces, axes, split_axis=0, concat_axis=0, tiled=True)  68.2 us
    all_gather x1, blocking collectives, body(): lax.all_gather(scaled, 'z_hi', axis=0, tiled=False, axis_index_groups=FIR...  10.3 us
    all_gather x1, blocking collectives, body(): lax.all_gather(scaled, ROW, axis=0, tiled=False, axis_index_groups=quads)  9.62 us
    all_to_all x1, waiting for transfers between devices, exchange(): return lax.all_to_all(pieces, axes, split_axis=0, concat_axis=0, tiled=True)  5.09 us
    all_to_all x1, starting transfers between devices, exchange(): return lax.all_to_all(pieces, axes, split_axis=0, concat_axis=0, tiled=True)  4.36 us
    pallas_call x1, Pallas kernels, body(): call(weight_grads, [shape(w.shape, BF16) for w in (gate_weight, up_weight...  2.53 us
    all_gather x1, blocking collectives, body(): both = lax.all_gather(partial, 'core', axis=0, tiled=False)  2.37 us
  transfers between devices with their start and end apart: 1, of which 1 were waited for; matrix products, arithmetic and copies ran while one was open for 0% of the time, Pallas kernels for 2%

profile of v10, /device:TPU:8, one launch (start us, length us, event | category | flops | bytes accessed | tf_op | source)
XLA Modules:
  0.0 107.2 jit_solution(10903424817241400978)
XLA Ops:
  0.6 0.8 pad_maximum_fusion
  1.4 14.5 %all_to_all.20.line_ref = bf16[4,8,2048]{2,1,0:T(8,128)(2,1)S(1)} all-to-all(bf16[4,8,2048]{2,1,0:T(8,128)(2,1)S(1)} %broadcast_in_dim.2), channel_id=1, replica_groups=mesh['z_lo'=2,'x'=4,'z_hi'=4,'core'=2,'y_hi'=4,'y_lo'=2] {'y_hi'}, dimensions={0} | all-to-all | bytes 262144 | tf_op jit(solution)/shard_map/all_to_all | solution.py:27
  15.9 0.2 shard_map.84
  16.1 0.0 copy-start
  16.1 0.0 copy-start.1
  16.1 0.0 copy-start.2
  16.1 32.1 %all_to_all.21.plane_ref = bf16[16,32,2048]{2,1,0:T(8,128)(2,1)S(1)} all-to-all(bf16[16,32,2048]{2,1,0:T(8,128)(2,1)S(1)} %shard_map.84), channel_id=1, replica_groups=mesh['z_lo'=2,'x'=4,'z_hi'=4,'core'=2,'y_hi'=4,'y_lo'=2] {'x','z_lo','y_..., dimensions={0} | all-to-all | bytes 4194304 | tf_op jit(solution)/shard_map/all_to_all | solution.py:27
  48.3 0.0 copy-done
  48.3 0.0 copy-done.1
  48.3 0.0 copy-done.2
  48.3 0.7 shard_map.85
  49.0 2.4 %all-gather = f32[512,384]{1,0:T(8,128)S(1)} all-gather(f32[256,384]{1,0:T(8,128)S(1)} %shard_map.85), channel_id=2, replica_groups=mesh['z_lo'=2,'x'=4,'z_hi'=4,'core'=2,'y_hi'=4,'y_lo'=2] {'core'}, dimensions={0}, use_global_device_ids=true | all-gather | bytes 1179648 | tf_op jit(solution)/shard_map/all_gather | solution.py:184
  51.3 0.1 shard_map.86
  51.4 10.3 %all-gather.1 = f16[272,384]{1,0:T(8,128)(2,1)S(1)} all-gather(f16[136,384]{1,0:T(8,128)(2,1)S(1)} %convert_element_type.14), channel_id=3, replica_groups={{0,16},{32,48},{1,17},{33,49},{2,18},{34,50},{3,19},{35,51},{4,20},{36,..., dimensions={0}, use_global_device_ids=true | all-gather | bytes 313344 | tf_op jit(solution)/shard_map/all_gather | solution.py:197
  61.8 0.1 shard_map.87
  61.9 9.6 %all-gather.2 = f16[544,384]{1,0:T(8,128)(2,1)S(1)} all-gather(f16[136,384]{1,0:T(8,128)(2,1)S(1)} %convert_element_type.16), channel_id=4, replica_groups={{0,8,48,56},{16,24,32,40},{1,9,49,57},{17,25,33,41},{2,10,50,58},{18,26..., dimensions={0}, use_global_device_ids=true | all-gather | bytes 522240 | tf_op jit(solution)/shard_map/all_gather | solution.py:200
  71.5 0.1 convert.2.parts_ref
  71.5 0.1 shard_map.88.triple_ref
  71.7 0.5 shard_map.89
  72.1 21.6 %all_to_all.22.pieces_ref = bf16[8,32,2048]{2,1,0:T(8,128)(2,1)S(1)} all-to-all(bf16[8,32,2048]{2,1,0:T(8,128)(2,1)S(1)} %shard_map.89), channel_id=1, replica_groups=mesh['z_lo'=2,'x'=4,'z_hi'=4,'core'=2,'y_hi'=4,'y_lo'=2] {'x','z_lo'}, dimensions={0} | all-to-all | bytes 2097152 | tf_op jit(solution)/shard_map/all_to_all | solution.py:27
  93.8 0.8 shard_map.90
  94.6 4.4 %all-to-all-start.3 = ((bf16[8,8,1024]{2,1,0:T(8,128)(2,1)}), bf16[8,8,1024]{2,1,0:T(8,128)(2,1)S(1)}, u32[]{:S(2)}, u32[]{:S(2)}) async-start(bf16[8,8,1024]{2,1,0:T(8,128)(2,1)} %bitcast.4), calls=%async_computation.3 | async-start | bytes 262144 | tf_op jit(solution)/shard_map/all_to_all | solution.py:27
  98.9 2.5 %shard_map.92 = (bf16[2048,128]{1,0:T(8,128)(2,1)}, bf16[2048,128]{1,0:T(8,128)(2,1)}, bf16[128,2048]{1,0:T(8,128)(2,1)}) custom-call(bf16[256,384]{1,0:T(8,128)(2,1)S(1)} %shard_map.88.triple_ref, bf16[16,32,2048]{2,1,0:T(8,128)(2,1)S(1)} %all_to_all.21.plane_ref), custom_call_target="tpu_custom_call" | custom-call | flops 402653184 | bytes 3670016 | tf_op jit(solution)/shard_map/pallas_call | solution.py:218
  101.5 5.1 %all-to-all-done.3.pieces_ref = bf16[8,8,1024]{2,1,0:T(8,128)(2,1)S(1)} async-done(((bf16[8,8,1024]{2,1,0:T(8,128)(2,1)}), bf16[8,8,1024]{2,1,0:T(8,128)(2,1)S(1)}, u32[]{:S(2)}, u32[]{:S(2)}) %all-to-all-start.3) | async-done | bytes 131104 | tf_op jit(solution)/shard_map/all_to_all | solution.py:27
  106.6 0.6 shard_map.91
  (4 shorter events, 0.1 us)
Async XLA Ops:
  16.1 32.2 %copy-start = (bf16[2048,128]{1,0:T(8,128)(2,1)S(1)}, bf16[2048,128]{1,0:T(8,128)(2,1)}, u32[]{:S(2)}) copy-start(bf16[2048,128]{1,0:T(8,128)(2,1)} %gate_ref.3) | copy-start | bytes 1572868
  16.1 32.2 %copy-start.1 = (bf16[2048,128]{1,0:T(8,128)(2,1)S(1)}, bf16[2048,128]{1,0:T(8,128)(2,1)}, u32[]{:S(2)}) copy-start(bf16[2048,128]{1,0:T(8,128)(2,1)} %up_ref.3) | copy-start | bytes 1572868
  16.1 32.2 %copy-start.2 = (bf16[128,2048]{1,0:T(8,128)(2,1)S(1)}, bf16[128,2048]{1,0:T(8,128)(2,1)}, u32[]{:S(2)}) copy-start(bf16[128,2048]{1,0:T(8,128)(2,1)} %down_ref.1) | copy-start | bytes 1572868
  94.6 12.0 %all-to-all-start.3 = ((bf16[8,8,1024]{2,1,0:T(8,128)(2,1)}), bf16[8,8,1024]{2,1,0:T(8,128)(2,1)S(1)}, u32[]{:S(2)}, u32[]{:S(2)}) async-start(bf16[8,8,1024]{2,1,0:T(8,128)(2,1)} %bitcast.4), calls=%async_computation.3 | async-start | bytes 262144 | tf_op jit(solution)/shard_map/all_to_all | solution.py:27

commit v11 on v10

--- a/solution.py
+++ b/solution.py
@@ -168,7 +168,8 @@
     block = jnp.concatenate([inputs, cotangent], axis=0)
     core = lax.axis_index("core").astype(jnp.int32).reshape(1)
     block, core = lax.optimization_barrier((block, core))
-    line = spread(block, "y_hi").reshape(groups // near, 2 * own, depth)
+    line = lax.all_gather(block, "y_hi", axis=0, tiled=False, axis_index_groups=FIRST_PAIRS)
+    line = lax.all_gather(line, "y_hi", axis=0, tiled=True, axis_index_groups=SECOND_PAIRS)
     copies = call(
         split_line,
         shape((near, rows, depth), BF16),

time: 108 us -> 108 us (level)
  starting transfers between devices: 4.36 us -> 6.78 us
  blocking collectives: 90.5 us -> 88.4 us
    all_to_all x3 -> x2, blocking collectives: 68.2 us -> 53.6 us  [exchange(): return lax.all_to_all(pieces, axes, split_axis=0, concat_axis=0, tiled=True)]
    all_gather x0 -> x2, blocking collectives: none -> 12.5 us  [the longest x1 7.04 us: body(): lax.all_gather(line, 'y_hi', axis=0, tiled=True, axis_index_groups=SECOND...]
    all_to_all x1, starting transfers between devices: 4.36 us -> 6.78 us  [exchange(): return lax.all_to_all(pieces, axes, split_axis=0, concat_axis=0, tiled=True)]
where the time goes in v11:
time: 108 us; the launch traced here: 107 us
  blocking collectives  88.4 us (82%)
  starting transfers between devices  6.78 us (6%)
  Pallas kernels  5.57 us (5%)
  waiting for transfers between devices  5.09 us (5%)
    all_to_all x2, blocking collectives, exchange(): return lax.all_to_all(pieces, axes, split_axis=0, concat_axis=0, tiled=True)  53.6 us
    all_gather x1, blocking collectives, body(): lax.all_gather(scaled, 'z_hi', axis=0, tiled=False, axis_index_groups=FIR...  10.3 us
    all_gather x1, blocking collectives, body(): lax.all_gather(scaled, ROW, axis=0, tiled=False, axis_index_groups=quads)  9.61 us
    all_gather x1, blocking collectives, body(): lax.all_gather(line, 'y_hi', axis=0, tiled=True, axis_index_groups=SECOND...  7.04 us
    all_to_all x1, starting transfers between devices, exchange(): return lax.all_to_all(pieces, axes, split_axis=0, concat_axis=0, tiled=True)  6.78 us
    all_gather x1, blocking collectives, body(): lax.all_gather(block, 'y_hi', axis=0, tiled=False, axis_index_groups=FIRS...  5.49 us
    all_to_all x1, waiting for transfers between devices, exchange(): return lax.all_to_all(pieces, axes, split_axis=0, concat_axis=0, tiled=True)  5.09 us
    pallas_call x1, Pallas kernels, body(): call(weight_grads, [shape(w.shape, BF16) for w in (gate_weight, up_weight...  2.53 us
  transfers between devices with their start and end apart: 1, of which 1 were waited for; matrix products, arithmetic and copies ran while one was open for 0% of the time, Pallas kernels for 2%

profile of v11, /device:TPU:8, one launch (start us, length us, event | category | flops | bytes accessed | tf_op | source)
XLA Modules:
  0.0 107.5 jit_solution(6566875390845016534)
XLA Ops:
  0.6 0.8 pad_maximum_fusion
  1.4 5.5 %all-gather = bf16[16,2048]{1,0:T(8,128)(2,1)S(1)} all-gather(bf16[8,2048]{1,0:T(8,128)(2,1)S(1)} %pad_maximum_fusion), channel_id=2, replica_groups={{0,2},{4,6},{1,3},{5,7},{8,10},{12,14},{9,11},{13,15},{16,18},{20,22},{..., dimensions={0}, use_global_device_ids=true | all-gather | bytes 98304 | tf_op jit(solution)/shard_map/all_gather | solution.py:171
  6.9 7.0 %all_gather.29.line_ref = bf16[4,8,2048]{2,1,0:T(8,128)(2,1)S(1)} all-gather(bf16[2,8,2048]{2,1,0:T(8,128)(2,1)S(1)} %bitcast.11), channel_id=1, replica_groups={{0,6},{2,4},{1,7},{3,5},{8,14},{10,12},{9,15},{11,13},{16,22},{18,20},{..., dimensions={0}, use_global_device_ids=true | all-gather | bytes 196608 | tf_op jit(solution)/shard_map/all_gather | solution.py:172
  13.9 0.2 shard_map.84
  14.1 0.0 copy-start
  14.1 0.0 copy-start.1
  14.2 0.0 copy-start.2
  14.2 32.0 %all_to_all.15.plane_ref = bf16[16,32,2048]{2,1,0:T(8,128)(2,1)S(1)} all-to-all(bf16[16,32,2048]{2,1,0:T(8,128)(2,1)S(1)} %shard_map.84), channel_id=1, replica_groups=mesh['z_lo'=2,'x'=4,'z_hi'=4,'core'=2,'y_hi'=4,'y_lo'=2] {'x','z_lo','y_..., dimensions={0} | all-to-all | bytes 4194304 | tf_op jit(solution)/shard_map/all_to_all | solution.py:27
  46.1 0.0 copy-done
  46.1 0.0 copy-done.1
  46.1 0.0 copy-done.2
  46.1 0.7 shard_map.85
  46.8 2.4 %all-gather.1 = f32[512,384]{1,0:T(8,128)S(1)} all-gather(f32[256,384]{1,0:T(8,128)S(1)} %shard_map.85), channel_id=3, replica_groups=mesh['z_lo'=2,'x'=4,'z_hi'=4,'core'=2,'y_hi'=4,'y_lo'=2] {'core'}, dimensions={0}, use_global_device_ids=true | all-gather | bytes 1179648 | tf_op jit(solution)/shard_map/all_gather | solution.py:185
  49.2 0.1 shard_map.86
  49.3 10.3 %all-gather.2 = f16[272,384]{1,0:T(8,128)(2,1)S(1)} all-gather(f16[136,384]{1,0:T(8,128)(2,1)S(1)} %convert_element_type.14), channel_id=4, replica_groups={{0,16},{32,48},{1,17},{33,49},{2,18},{34,50},{3,19},{35,51},{4,20},{36,..., dimensions={0}, use_global_device_ids=true | all-gather | bytes 313344 | tf_op jit(solution)/shard_map/all_gather | solution.py:198
  59.6 0.1 shard_map.87
  59.7 9.6 %all-gather.3 = f16[544,384]{1,0:T(8,128)(2,1)S(1)} all-gather(f16[136,384]{1,0:T(8,128)(2,1)S(1)} %convert_element_type.16), channel_id=5, replica_groups={{0,8,48,56},{16,24,32,40},{1,9,49,57},{17,25,33,41},{2,10,50,58},{18,26..., dimensions={0}, use_global_device_ids=true | all-gather | bytes 522240 | tf_op jit(solution)/shard_map/all_gather | solution.py:201
  69.3 0.1 convert.2.parts_ref
  69.4 0.1 shard_map.88.triple_ref
  69.5 0.5 shard_map.89
  70.0 21.6 %all_to_all.16.pieces_ref = bf16[8,32,2048]{2,1,0:T(8,128)(2,1)S(1)} all-to-all(bf16[8,32,2048]{2,1,0:T(8,128)(2,1)S(1)} %shard_map.89), channel_id=1, replica_groups=mesh['z_lo'=2,'x'=4,'z_hi'=4,'core'=2,'y_hi'=4,'y_lo'=2] {'x','z_lo'}, dimensions={0} | all-to-all | bytes 2097152 | tf_op jit(solution)/shard_map/all_to_all | solution.py:27
  91.7 0.8 shard_map.90
  92.5 6.8 %all-to-all-start.2 = ((bf16[8,8,1024]{2,1,0:T(8,128)(2,1)}), bf16[8,8,1024]{2,1,0:T(8,128)(2,1)S(1)}, u32[]{:S(2)}, u32[]{:S(2)}) async-start(bf16[8,8,1024]{2,1,0:T(8,128)(2,1)} %bitcast.5), calls=%async_computation.2 | async-start | bytes 262144 | tf_op jit(solution)/shard_map/all_to_all | solution.py:27
  99.2 2.5 %shard_map.92 = (bf16[2048,128]{1,0:T(8,128)(2,1)}, bf16[2048,128]{1,0:T(8,128)(2,1)}, bf16[128,2048]{1,0:T(8,128)(2,1)}) custom-call(bf16[256,384]{1,0:T(8,128)(2,1)S(1)} %shard_map.88.triple_ref, bf16[16,32,2048]{2,1,0:T(8,128)(2,1)S(1)} %all_to_all.15.plane_ref), custom_call_target="tpu_custom_call" | custom-call | flops 402653184 | bytes 3670016 | tf_op jit(solution)/shard_map/pallas_call | solution.py:219
  101.8 5.1 %all-to-all-done.2.pieces_ref = bf16[8,8,1024]{2,1,0:T(8,128)(2,1)S(1)} async-done(((bf16[8,8,1024]{2,1,0:T(8,128)(2,1)}), bf16[8,8,1024]{2,1,0:T(8,128)(2,1)S(1)}, u32[]{:S(2)}, u32[]{:S(2)}) %all-to-all-start.2) | async-done | bytes 131104 | tf_op jit(solution)/shard_map/all_to_all | solution.py:27
  106.9 0.6 shard_map.91
  (3 shorter events, 0.1 us)
Async XLA Ops:
  14.1 32.0 %copy-start = (bf16[2048,128]{1,0:T(8,128)(2,1)S(1)}, bf16[2048,128]{1,0:T(8,128)(2,1)}, u32[]{:S(2)}) copy-start(bf16[2048,128]{1,0:T(8,128)(2,1)} %gate_ref.3) | copy-start | bytes 1572868
  14.1 32.0 %copy-start.1 = (bf16[2048,128]{1,0:T(8,128)(2,1)S(1)}, bf16[2048,128]{1,0:T(8,128)(2,1)}, u32[]{:S(2)}) copy-start(bf16[2048,128]{1,0:T(8,128)(2,1)} %up_ref.3) | copy-start | bytes 1572868
  14.2 32.0 %copy-start.2 = (bf16[128,2048]{1,0:T(8,128)(2,1)S(1)}, bf16[128,2048]{1,0:T(8,128)(2,1)}, u32[]{:S(2)}) copy-start(bf16[128,2048]{1,0:T(8,128)(2,1)} %down_ref.1) | copy-start | bytes 1572868
  92.5 14.4 %all-to-all-start.2 = ((bf16[8,8,1024]{2,1,0:T(8,128)(2,1)}), bf16[8,8,1024]{2,1,0:T(8,128)(2,1)S(1)}, u32[]{:S(2)}, u32[]{:S(2)}) async-start(bf16[8,8,1024]{2,1,0:T(8,128)(2,1)} %bitcast.5), calls=%async_computation.2 | async-start | bytes 262144 | tf_op jit(solution)/shard_map/all_to_all | solution.py:27
